TPU v7x, 512 devices: a whole 4x8x8 slice. The times are simulated.
512 devices in a mesh: leaf: 512 (over z, y, x, core).
Axes of the slice: x: 4, y: 8, z: 8, core: 2. Of those that a mesh axis runs over, the one named last changes fastest.
Arguments:
- coords: bfloat16 [3, 2621440], P(None, 'leaf'), may hold values from 0 to 1
- rhs: float32 [8, 2621440], P(None, 'leaf'), may hold values from -6 to 6
- leaf_basis: bfloat16 [20480, 64, 128], P('leaf'), may hold values from -0.5 to 0.5
- leaf_transfer: bfloat16 [20480, 64, 64], P('leaf'), may hold values from -0.375 to 0.375
- upper_transfer: bfloat16 [512, 3, 64, 64], P('leaf'), may hold values from -0.25 to 0.25
- upper_coupling: bfloat16 [512, 4, 4, 64, 64], P('leaf'), may hold values from -0.1875 to 0.1875
- leaf_coupling: bfloat16 [20480, 8, 64, 64], P('leaf'), may hold values from -0.25 to 0.25
- near_lists: int32 [20480, 27], P('leaf'), may hold values from 0 to 199, as said below
- near_counts: int32 [20480], P('leaf'), may hold values from 1 to 27, as said below
- far_lists: int32 [20480, 8], P('leaf'), may hold values from 0 to 199, as said below
Outputs:
- product: float32 [8, 2621440], P(None, 'leaf')
Inputs may be any that keep to these rules, and one draw needn't show every extreme that they name: `near_lists`: window indices lie within 80 of the leaf's own window index 80 + (i % 40); slot 0 is the leaf itself; both ends of the window are reached. `near_counts`: some leaf uses every slot. `far_lists`: window indices lie within 80 of the leaf's own window index and never equal it; both ends of the window are reached.
All inputs are finite; a program needn't handle non-finite values.
Results may differ from a plain program's by a relative error of at most 0.0041.
Values may be sent and summed in bfloat16 or wider, within the bound.
A program may use at most 64 MiB of HBM per device.

v0:
```python
import jax
import jax.numpy as jnp
from jax import lax
from jax.sharding import PartitionSpec as P

LENGTH_SCALE = 0.2
NOISE = 0.1
box_offsets = (-3, -2, 2, 3)
window_offsets = (-2, -1, 1, 2)


def shifted(value, axis, steps):
    count = lax.axis_size(axis)
    initial, last = (max(0, -steps), min(count, count - steps))
    return lax.ppermute(value, axis, [(source, source + steps) for source in range(initial, last)])


def partner_2(block, axis, apart):
    count = lax.axis_size(axis)
    route = []
    for low in range(count):
        high = low | 1 << apart
        if high != low and high < count:
            route += [(low, high), (high, low)]
    return lax.ppermute(block, axis, route)


def matern(first, second):
    first = first.astype(jnp.float32)
    second = second.astype(jnp.float32)
    squared = jnp.zeros((first.shape[1], first.shape[2], second.shape[2]), jnp.float32)
    for axis_num in range(3):
        differ = first[axis_num][:, :, None] - second[axis_num][:, None, :]
        squared = squared + differ * differ
    scaled = jnp.sqrt(squared) * (3.0**0.5 / LENGTH_SCALE)
    return (1.0 + scaled) * jnp.exp(-scaled)


def leaf_coefs(rhs_leaf, basis):
    return jnp.einsum("alp,lrp->lar", rhs_leaf, basis, preferred_element_type=jnp.float32).astype(
        jnp.bfloat16
    )


def per_device(
    coords,
    rhs,
    leaf_basis,
    leaf_transfer,
    upper_transfer,
    upper_coupling,
    leaf_coupling,
    near_lists,
    near_counts,
    far_lists,
):
    leaves = leaf_basis.shape[0]
    rank = leaf_basis.shape[1]
    leaf = leaf_basis.shape[2]
    nrhs = rhs.shape[0]
    levels_up = upper_transfer.shape[1]
    rhs_leaf = rhs.astype(jnp.bfloat16).reshape(nrhs, leaves, leaf)
    own_points = coords.reshape(3, leaves, leaf)
    coef = leaf_coefs(rhs_leaf, leaf_basis)
    received = {}
    for offset in window_offsets:
        received[offset] = shifted((own_points, rhs_leaf, coef), "leaf", -offset)
    received[0] = (own_points, rhs_leaf, coef)
    ordered = [received[offset] for offset in (-2, -1, 0, 1, 2)]
    coord_win = jnp.concatenate([piece[0] for piece in ordered], axis=1)
    rhs_win = jnp.concatenate([piece[1] for piece in ordered], axis=1)
    coef_win = jnp.concatenate([piece[2] for piece in ordered], axis=0)
    level_zero = jnp.einsum(
        "lar,lrs->as", coef, leaf_transfer, preferred_element_type=jnp.float32
    ).astype(jnp.bfloat16)
    lifted = jnp.einsum(
        "as,jst->jat", level_zero, upper_transfer[0], preferred_element_type=jnp.float32
    )
    up_terms = jnp.concatenate([level_zero.astype(jnp.float32)[None], lifted], axis=0)
    local = jnp.zeros((nrhs, rank), jnp.float32)
    running = up_terms
    for bit_num in range(levels_up):
        partner = partner_2(running[bit_num + 1 :], "leaf", bit_num)
        running = jnp.concatenate(
            [running[: bit_num + 1], running[bit_num + 1 :] + partner], axis=0
        )
    levels = running.astype(jnp.bfloat16)
    for level in range(levels_up + 1):
        for number, offset in enumerate(box_offsets):
            box_coef = shifted(levels[level], "leaf", -offset * 2**level)
            local = local + jnp.dot(
                box_coef, upper_coupling[0, level, number], preferred_element_type=jnp.float32
            )
    local = local.astype(jnp.bfloat16)
    far_coef = jnp.take(coef_win, far_lists, axis=0)
    leaf_local = jnp.einsum(
        "lkar,lkrs->las", far_coef, leaf_coupling, preferred_element_type=jnp.float32
    )
    leaf_local = leaf_local + jnp.einsum(
        "lrs,as->lar", leaf_transfer, local, preferred_element_type=jnp.float32
    )
    leaf_local = leaf_local.astype(jnp.bfloat16)
    far = jnp.einsum("lar,lrp->alp", leaf_local, leaf_basis, preferred_element_type=jnp.float32)

    def one_slot(column, summed):
        chosen = near_lists[:, column]
        others = jnp.take(coord_win, chosen, axis=1)
        block = matern(own_points, others).astype(jnp.bfloat16)
        sources = jnp.take(rhs_win, chosen, axis=1)
        term = jnp.einsum("lpq,alq->alp", block, sources, preferred_element_type=jnp.float32)
        live = (column < near_counts).astype(jnp.float32)
        return summed + term * live[None, :, None]

    upper_end = near_lists.shape[1]
    near = lax.fori_loop(0, upper_end, one_slot, jnp.zeros((nrhs, leaves, leaf), jnp.float32))
    result = near + far + NOISE * rhs.reshape(nrhs, leaves, leaf)
    return result.reshape(nrhs, leaves * leaf)


def solution(mesh):
    return jax.shard_map(
        per_device,
        mesh=mesh,
        in_specs=(
            P(None, "leaf"),
            P(None, "leaf"),
            P("leaf", None, None),
            P("leaf", None, None),
            P("leaf", None, None, None),
            P("leaf", None, None, None, None),
            P("leaf", None, None, None),
            P("leaf", None),
            P("leaf"),
            P("leaf", None),
        ),
        out_specs=P(None, "leaf"),
        check_vma=False,
    )
```

profile of v0, /device:TPU:255, one launch (start us, length us, event | category | flops | bytes accessed | tf_op | source)
XLA Modules:
  0.0 413.1 jit_solution(10142082440167634807)
XLA Ops:
  1.0 4.3 %collective-permute-start = (bf16[8,40,128]{2,0,1:T(8,128)(2,1)S(1)}, bf16[8,40,128]{2,0,1:T(8,128)(2,1)S(1)}, u32[]{:S(2)}, u32[]{:S(2)}) collective-permute-start(bf16[8,40,128]{2,0,1:T(8,128)(2,1)S(1)} %convert_bitcast_fusion.1), channel_id=1, source_target_pairs={{0,2},{1,3},{2,4},{3,5},{4,6},{5,7},{6,8},{7,9},{8,10},{9,11},{10,... | collective-permute-start | bytes 245768 | tf_op jit(solution)/shard_map/ppermute | solution.py:15
  5.3 4.0 collective-permute-start.1
  20.6 6.1 %collective-permute-done.15 = bf16[8,64]{1,0:T(8,128)(2,1)S(1)} collective-permute-done((bf16[8,64]{1,0:T(8,128)(2,1)S(1)}, bf16[8,64]{1,0:T(8,128)(2,1)S(1)}, u32[]{:S(2)}, u32[]{:S(2)}) %collective-permute-start.15) | collective-permute-done | bytes 1056 | tf_op jit(solution)/shard_map/ppermute | solution.py:15
  29.5 7.0 %collective-permute-done.14 = bf16[8,64]{1,0:T(8,128)(2,1)S(1)} collective-permute-done((bf16[8,64]{1,0:T(8,128)(2,1)S(1)}, bf16[8,64]{1,0:T(8,128)(2,1)S(1)}, u32[]{:S(2)}, u32[]{:S(2)}) %collective-permute-start.14) | collective-permute-done | bytes 1056 | tf_op jit(solution)/shard_map/ppermute | solution.py:15
  46.7 5.8 %collective-permute-done.20 = bf16[8,64]{1,0:T(8,128)(2,1)S(1)} collective-permute-done((bf16[8,64]{1,0:T(8,128)(2,1)S(1)}, bf16[8,64]{1,0:T(8,128)(2,1)S(1)}, u32[]{:S(2)}, u32[]{:S(2)}) %collective-permute-start.20) | collective-permute-done | bytes 1056 | tf_op jit(solution)/shard_map/ppermute | solution.py:15
  56.1 6.3 %collective-permute-done.19 = bf16[8,64]{1,0:T(8,128)(2,1)S(1)} collective-permute-done((bf16[8,64]{1,0:T(8,128)(2,1)S(1)}, bf16[8,64]{1,0:T(8,128)(2,1)S(1)}, u32[]{:S(2)}, u32[]{:S(2)}) %collective-permute-start.19) | collective-permute-done | bytes 1056 | tf_op jit(solution)/shard_map/ppermute | solution.py:15
  81.1 8.2 %collective-permute-done.25 = bf16[8,64]{1,0:T(8,128)(2,1)S(1)} collective-permute-done((bf16[8,64]{1,0:T(8,128)(2,1)S(1)}, bf16[8,64]{1,0:T(8,128)(2,1)S(1)}, u32[]{:S(2)}, u32[]{:S(2)}) %collective-permute-start.25) | collective-permute-done | bytes 1056 | tf_op jit(solution)/shard_map/ppermute | solution.py:15
  92.2 4.9 %collective-permute-done.24 = bf16[8,64]{1,0:T(8,128)(2,1)S(1)} collective-permute-done((bf16[8,64]{1,0:T(8,128)(2,1)S(1)}, bf16[8,64]{1,0:T(8,128)(2,1)S(1)}, u32[]{:S(2)}, u32[]{:S(2)}) %collective-permute-start.24) | collective-permute-done | bytes 1056 | tf_op jit(solution)/shard_map/ppermute | solution.py:15
  109.2 4.8 %collective-permute-done.22 = bf16[8,64]{1,0:T(8,128)(2,1)S(1)} collective-permute-done((bf16[8,64]{1,0:T(8,128)(2,1)S(1)}, bf16[8,64]{1,0:T(8,128)(2,1)S(1)}, u32[]{:S(2)}, u32[]{:S(2)}) %collective-permute-start.22) | collective-permute-done | bytes 1056 | tf_op jit(solution)/shard_map/ppermute | solution.py:15
  116.8 6.7 %collective-permute-done.30 = bf16[8,64]{1,0:T(8,128)(2,1)S(1)} collective-permute-done((bf16[8,64]{1,0:T(8,128)(2,1)S(1)}, bf16[8,64]{1,0:T(8,128)(2,1)S(1)}, u32[]{:S(2)}, u32[]{:S(2)}) %collective-permute-start.30) | collective-permute-done | bytes 1056 | tf_op jit(solution)/shard_map/ppermute | solution.py:15
  123.4 4.1 collective-permute-start.29
  143.3 26.0 %collective-permute-start.12 = (bf16[8,64]{1,0:T(8,128)(2,1)S(1)}, bf16[8,64]{1,0:T(8,128)(2,1)S(1)}, u32[]{:S(2)}, u32[]{:S(2)}) collective-permute-start(bf16[8,64]{1,0:T(8,128)(2,1)S(1)} %fusion.27), channel_id=1, source_target_pairs={{0,3},{1,4},{2,5},{3,6},{4,7},{5,8},{6,9},{7,10},{8,11},{9,12},{10... | collective-permute-start | bytes 3080 | tf_op jit(solution)/shard_map/ppermute | solution.py:15
  170.1 3.8 collective-permute-start.4
  175.4 15.6 %collective-permute-start.5 = (bf16[3,40,128]{2,0,1:T(4,128)(2,1)}, bf16[3,40,128]{2,0,1:T(4,128)(2,1)S(1)}, u32[]{:S(2)}, u32[]{:S(2)}) collective-permute-start(bf16[3,40,128]{2,0,1:T(4,128)(2,1)} %bitcast.172), channel_id=1, source_target_pairs={{0,1},{1,2},{2,3},{3,4},{4,5},{5,6},{6,7},{7,8},{8,9},{9,10},{10,1... | collective-permute-start | bytes 92168 | tf_op jit(solution)/shard_map/ppermute | solution.py:15
  194.4 9.2 %collective-permute-done.6 = bf16[3,40,128]{2,0,1:T(4,128)(2,1)S(1)} collective-permute-done((bf16[3,40,128]{2,0,1:T(4,128)(2,1)S(1)}, bf16[3,40,128]{2,0,1:T(4,128)(2,1)S(1)}, u32[]{:S(2)}, u32[]{:S(2)}) %collective-permute-start.6) | collective-permute-done | bytes 30752 | tf_op jit(solution)/shard_map/ppermute | solution.py:15
  205.6 8.2 %collective-permute-done.7 = bf16[3,40,128]{2,0,1:T(4,128)(2,1)S(1)} collective-permute-done((bf16[3,40,128]{2,0,1:T(4,128)(2,1)S(1)}, bf16[3,40,128]{2,0,1:T(4,128)(2,1)S(1)}, u32[]{:S(2)}, u32[]{:S(2)}) %collective-permute-start.7) | collective-permute-done | bytes 30752 | tf_op jit(solution)/shard_map/ppermute | solution.py:15
  219.0 4.2 %collective-permute-start.9 = (bf16[40,8,64]{2,1,0:T(8,128)(2,1)S(1)}, bf16[40,8,64]{2,1,0:T(8,128)(2,1)S(1)}, u32[]{:S(2)}, u32[]{:S(2)}) collective-permute-start(bf16[40,8,64]{2,1,0:T(8,128)(2,1)S(1)} %convolution_convert_fusion), channel_id=1, source_target_pairs={{0,1},{1,2},{2,3},{3,4},{4,5},{5,6},{6,7},{7,8},{8,9},{9,10},{10,1... | collective-permute-start | bytes 122888 | tf_op jit(solution)/shard_map/ppermute | solution.py:15
  226.6 9.9 %collective-permute-done.10 = bf16[40,8,64]{2,1,0:T(8,128)(2,1)S(1)} collective-permute-done((bf16[40,8,64]{2,1,0:T(8,128)(2,1)S(1)}, bf16[40,8,64]{2,1,0:T(8,128)(2,1)S(1)}, u32[]{:S(2)}, u32[]{:S(2)}) %collective-permute-start.10) | collective-permute-done | bytes 40992 | tf_op jit(solution)/shard_map/ppermute | solution.py:15
  238.4 8.7 %collective-permute-done.11 = bf16[40,8,64]{2,1,0:T(8,128)(2,1)S(1)} collective-permute-done((bf16[40,8,64]{2,1,0:T(8,128)(2,1)S(1)}, bf16[40,8,64]{2,1,0:T(8,128)(2,1)S(1)}, u32[]{:S(2)}, u32[]{:S(2)}) %collective-permute-start.11) | collective-permute-done | bytes 40992 | tf_op jit(solution)/shard_map/ppermute | solution.py:15
  253.2 159.2 %while.14 = (s32[]{:T(128)}, f32[8,40,128]{2,0,1:T(8,128)S(1)}, s32[40,27]{0,1:T(8,128)}, bf16[8,200,128]{2,0,1:T(8,128)(2,1)S(1)}, bf16[3,40,128]{2,1,0:T(8,128...) while((s32[]{:T(128)}, f32[8,40,128]{2,0,1:T(8,128)S(1)}, ...), condition=%wide.region_1.2_spmd.clone, body=%wide.region_0.1_spmd.clone.sunk | while | flops 19216708 | bytes 1193455 | solution.py:115
  255.4 3.7 fusion.117
  261.3 3.7 fusion.117
  267.2 3.7 fusion.117
  279.0 3.7 fusion.117
  326.1 3.7 fusion.117
  332.0 3.7 fusion.117
  373.3 3.7 fusion.117
  379.2 3.7 fusion.117
  385.1 3.7 fusion.117
  391.0 3.7 fusion.117
  396.9 3.7 fusion.117
  402.8 3.7 fusion.117
  (365 shorter events, 218.8 us)
Async XLA Ops:
  0.0 192.4 %copy-start.3 = (bf16[3,5120]{1,0:T(4,128)(2,1)S(1)}, bf16[3,5120]{1,0:T(4,128)(2,1)}, u32[]{:S(2)}) copy-start(bf16[3,5120]{1,0:T(4,128)(2,1)} %param.12) | copy-start | bytes 92164
  1.0 252.0 %collective-permute-start = (bf16[8,40,128]{2,0,1:T(8,128)(2,1)S(1)}, bf16[8,40,128]{2,0,1:T(8,128)(2,1)S(1)}, u32[]{:S(2)}, u32[]{:S(2)}) collective-permute-start(bf16[8,40,128]{2,0,1:T(8,128)(2,1)S(1)} %convert_bitcast_fusion.1), channel_id=1, source_target_pairs={{0,2},{1,3},{2,4},{3,5},{4,6},{5,7},{6,8},{7,9},{8,10},{9,11},{10,... | collective-permute-start | bytes 245768 | tf_op jit(solution)/shard_map/ppermute | solution.py:15
  5.3 247.7 %collective-permute-start.1 = (bf16[8,40,128]{2,0,1:T(8,128)(2,1)S(1)}, bf16[8,40,128]{2,0,1:T(8,128)(2,1)S(1)}, u32[]{:S(2)}, u32[]{:S(2)}) collective-permute-start(bf16[8,40,128]{2,0,1:T(8,128)(2,1)S(1)} %convert_bitcast_fusion.1), channel_id=1, source_target_pairs={{0,1},{1,2},{2,3},{3,4},{4,5},{5,6},{6,7},{7,8},{8,9},{9,10},{10,1... | collective-permute-start | bytes 245768 | tf_op jit(solution)/shard_map/ppermute | solution.py:15
  9.3 243.8 %collective-permute-start.2 = (bf16[8,40,128]{2,0,1:T(8,128)(2,1)S(1)}, bf16[8,40,128]{2,0,1:T(8,128)(2,1)S(1)}, u32[]{:S(2)}, u32[]{:S(2)}) collective-permute-start(bf16[8,40,128]{2,0,1:T(8,128)(2,1)S(1)} %convert_bitcast_fusion.1), channel_id=1, source_target_pairs={{1,0},{2,1},{3,2},{4,3},{5,4},{6,5},{7,6},{8,7},{9,8},{10,9},{11,1... | collective-permute-start | bytes 245768 | tf_op jit(solution)/shard_map/ppermute | solution.py:15
  11.2 241.9 %collective-permute-start.3 = (bf16[8,40,128]{2,0,1:T(8,128)(2,1)S(1)}, bf16[8,40,128]{2,0,1:T(8,128)(2,1)S(1)}, u32[]{:S(2)}, u32[]{:S(2)}) collective-permute-start(bf16[8,40,128]{2,0,1:T(8,128)(2,1)S(1)} %convert_bitcast_fusion.1), channel_id=1, source_target_pairs={{2,0},{3,1},{4,2},{5,3},{6,4},{7,5},{8,6},{9,7},{10,8},{11,9},{12,... | collective-permute-start | bytes 245768 | tf_op jit(solution)/shard_map/ppermute | solution.py:15
  15.2 11.5 %collective-permute-start.15 = (bf16[8,64]{1,0:T(8,128)(2,1)S(1)}, bf16[8,64]{1,0:T(8,128)(2,1)S(1)}, u32[]{:S(2)}, u32[]{:S(2)}) collective-permute-start(bf16[8,64]{1,0:T(8,128)(2,1)S(1)} %fusion.27), channel_id=1, source_target_pairs={{3,0},{4,1},{5,2},{6,3},{7,4},{8,5},{9,6},{10,7},{11,8},{12,9},{13... | collective-permute-start | bytes 3080 | tf_op jit(solution)/shard_map/ppermute | solution.py:15
  26.7 9.7 %collective-permute-start.14 = (bf16[8,64]{1,0:T(8,128)(2,1)S(1)}, bf16[8,64]{1,0:T(8,128)(2,1)S(1)}, u32[]{:S(2)}, u32[]{:S(2)}) collective-permute-start(bf16[8,64]{1,0:T(8,128)(2,1)S(1)} %fusion.27), channel_id=1, source_target_pairs={{2,0},{3,1},{4,2},{5,3},{6,4},{7,5},{8,6},{9,7},{10,8},{11,9},{12,... | collective-permute-start | bytes 3080 | tf_op jit(solution)/shard_map/ppermute | solution.py:15
  36.5 3.1 collective-permute-start.16
  39.6 4.3 %collective-permute-start.13 = (bf16[8,64]{1,0:T(8,128)(2,1)S(1)}, bf16[8,64]{1,0:T(8,128)(2,1)S(1)}, u32[]{:S(2)}, u32[]{:S(2)}) collective-permute-start(bf16[8,64]{1,0:T(8,128)(2,1)S(1)} %fusion.27), channel_id=1, source_target_pairs={{0,2},{1,3},{2,4},{3,5},{4,6},{5,7},{6,8},{7,9},{8,10},{9,11},{10,... | collective-permute-start | bytes 3080 | tf_op jit(solution)/shard_map/ppermute | solution.py:15
  43.9 8.5 %collective-permute-start.20 = (bf16[8,64]{1,0:T(8,128)(2,1)S(1)}, bf16[8,64]{1,0:T(8,128)(2,1)S(1)}, u32[]{:S(2)}, u32[]{:S(2)}) collective-permute-start(bf16[8,64]{1,0:T(8,128)(2,1)S(1)} %fusion.83), channel_id=1, source_target_pairs={{6,0},{7,1},{8,2},{9,3},{10,4},{11,5},{12,6},{13,7},{14,8},{15,9},... | collective-permute-start | bytes 3080 | tf_op jit(solution)/shard_map/ppermute | solution.py:15
  52.4 10.0 %collective-permute-start.19 = (bf16[8,64]{1,0:T(8,128)(2,1)S(1)}, bf16[8,64]{1,0:T(8,128)(2,1)S(1)}, u32[]{:S(2)}, u32[]{:S(2)}) collective-permute-start(bf16[8,64]{1,0:T(8,128)(2,1)S(1)} %fusion.83), channel_id=1, source_target_pairs={{4,0},{5,1},{6,2},{7,3},{8,4},{9,5},{10,6},{11,7},{12,8},{13,9},{1... | collective-permute-start | bytes 3080 | tf_op jit(solution)/shard_map/ppermute | solution.py:15
  62.5 5.8 %collective-permute-start.18 = (bf16[8,64]{1,0:T(8,128)(2,1)S(1)}, bf16[8,64]{1,0:T(8,128)(2,1)S(1)}, u32[]{:S(2)}, u32[]{:S(2)}) collective-permute-start(bf16[8,64]{1,0:T(8,128)(2,1)S(1)} %fusion.83), channel_id=1, source_target_pairs={{0,4},{1,5},{2,6},{3,7},{4,8},{5,9},{6,10},{7,11},{8,12},{9,13},{1... | collective-permute-start | bytes 3080 | tf_op jit(solution)/shard_map/ppermute | solution.py:15
  68.3 4.5 %collective-permute-start.21 = (f32[2,8,64]{2,1,0:T(8,128)S(1)}, f32[2,8,64]{2,1,0:T(8,128)S(1)}, u32[]{:S(2)}, u32[]{:S(2)}) collective-permute-start(f32[2,8,64]{2,1,0:T(8,128)S(1)} %slice.176), channel_id=1, source_target_pairs={{0,2},{2,0},{1,3},{3,1},{4,6},{6,4},{5,7},{7,5},{8,10},{10,8},{9,1... | collective-permute-start | bytes 12296 | tf_op jit(solution)/shard_map/ppermute | solution.py:25
  72.8 5.5 %collective-permute-start.17 = (bf16[8,64]{1,0:T(8,128)(2,1)S(1)}, bf16[8,64]{1,0:T(8,128)(2,1)S(1)}, u32[]{:S(2)}, u32[]{:S(2)}) collective-permute-start(bf16[8,64]{1,0:T(8,128)(2,1)S(1)} %fusion.83), channel_id=1, source_target_pairs={{0,6},{1,7},{2,8},{3,9},{4,10},{5,11},{6,12},{7,13},{8,14},{9,15},... | collective-permute-start | bytes 3080 | tf_op jit(solution)/shard_map/ppermute | solution.py:15
  78.3 10.9 %collective-permute-start.25 = (bf16[8,64]{1,0:T(8,128)(2,1)S(1)}, bf16[8,64]{1,0:T(8,128)(2,1)S(1)}, u32[]{:S(2)}, u32[]{:S(2)}) collective-permute-start(bf16[8,64]{1,0:T(8,128)(2,1)S(1)} %fusion.84), channel_id=1, source_target_pairs={{12,0},{13,1},{14,2},{15,3},{16,4},{17,5},{18,6},{19,7},{20,8},{21... | collective-permute-start | bytes 3080 | tf_op jit(solution)/shard_map/ppermute | solution.py:15
  89.3 7.8 %collective-permute-start.24 = (bf16[8,64]{1,0:T(8,128)(2,1)S(1)}, bf16[8,64]{1,0:T(8,128)(2,1)S(1)}, u32[]{:S(2)}, u32[]{:S(2)}) collective-permute-start(bf16[8,64]{1,0:T(8,128)(2,1)S(1)} %fusion.84), channel_id=1, source_target_pairs={{8,0},{9,1},{10,2},{11,3},{12,4},{13,5},{14,6},{15,7},{16,8},{17,9... | collective-permute-start | bytes 3080 | tf_op jit(solution)/shard_map/ppermute | solution.py:15
  97.1 4.3 %collective-permute-start.23 = (bf16[8,64]{1,0:T(8,128)(2,1)S(1)}, bf16[8,64]{1,0:T(8,128)(2,1)S(1)}, u32[]{:S(2)}, u32[]{:S(2)}) collective-permute-start(bf16[8,64]{1,0:T(8,128)(2,1)S(1)} %fusion.84), channel_id=1, source_target_pairs={{0,8},{1,9},{2,10},{3,11},{4,12},{5,13},{6,14},{7,15},{8,16},{9,17... | collective-permute-start | bytes 3080 | tf_op jit(solution)/shard_map/ppermute | solution.py:15
  101.4 5.8 %collective-permute-start.26 = (f32[1,8,64]{2,1,0:T(8,128)S(1)}, f32[1,8,64]{2,1,0:T(8,128)S(1)}, u32[]{:S(2)}, u32[]{:S(2)}) collective-permute-start(f32[1,8,64]{2,1,0:T(8,128)S(1)} %slice.178), channel_id=1, source_target_pairs={{0,4},{4,0},{1,5},{5,1},{2,6},{6,2},{3,7},{7,3},{8,12},{12,8},{9,1... | collective-permute-start | bytes 6152 | tf_op jit(solution)/shard_map/ppermute | solution.py:25
  107.3 6.7 %collective-permute-start.22 = (bf16[8,64]{1,0:T(8,128)(2,1)S(1)}, bf16[8,64]{1,0:T(8,128)(2,1)S(1)}, u32[]{:S(2)}, u32[]{:S(2)}) collective-permute-start(bf16[8,64]{1,0:T(8,128)(2,1)S(1)} %fusion.84), channel_id=1, source_target_pairs={{0,12},{1,13},{2,14},{3,15},{4,16},{5,17},{6,18},{7,19},{8,20},{9,... | collective-permute-start | bytes 3080 | tf_op jit(solution)/shard_map/ppermute | solution.py:15
  114.0 9.4 %collective-permute-start.30 = (bf16[8,64]{1,0:T(8,128)(2,1)S(1)}, bf16[8,64]{1,0:T(8,128)(2,1)S(1)}, u32[]{:S(2)}, u32[]{:S(2)}) collective-permute-start(bf16[8,64]{1,0:T(8,128)(2,1)S(1)} %fusion.82), channel_id=1, source_target_pairs={{24,0},{25,1},{26,2},{27,3},{28,4},{29,5},{30,6},{31,7},{32,8},{33... | collective-permute-start | bytes 3080 | tf_op jit(solution)/shard_map/ppermute | solution.py:15
  123.4 8.5 %collective-permute-start.29 = (bf16[8,64]{1,0:T(8,128)(2,1)S(1)}, bf16[8,64]{1,0:T(8,128)(2,1)S(1)}, u32[]{:S(2)}, u32[]{:S(2)}) collective-permute-start(bf16[8,64]{1,0:T(8,128)(2,1)S(1)} %fusion.82), channel_id=1, source_target_pairs={{16,0},{17,1},{18,2},{19,3},{20,4},{21,5},{22,6},{23,7},{24,8},{25... | collective-permute-start | bytes 3080 | tf_op jit(solution)/shard_map/ppermute | solution.py:15
  132.0 5.2 %collective-permute-start.28 = (bf16[8,64]{1,0:T(8,128)(2,1)S(1)}, bf16[8,64]{1,0:T(8,128)(2,1)S(1)}, u32[]{:S(2)}, u32[]{:S(2)}) collective-permute-start(bf16[8,64]{1,0:T(8,128)(2,1)S(1)} %fusion.82), channel_id=1, source_target_pairs={{0,16},{1,17},{2,18},{3,19},{4,20},{5,21},{6,22},{7,23},{8,24},{9,... | collective-permute-start | bytes 3080 | tf_op jit(solution)/shard_map/ppermute | solution.py:15
  137.2 6.1 %collective-permute-start.27 = (bf16[8,64]{1,0:T(8,128)(2,1)S(1)}, bf16[8,64]{1,0:T(8,128)(2,1)S(1)}, u32[]{:S(2)}, u32[]{:S(2)}) collective-permute-start(bf16[8,64]{1,0:T(8,128)(2,1)S(1)} %fusion.82), channel_id=1, source_target_pairs={{0,24},{1,25},{2,26},{3,27},{4,28},{5,29},{6,30},{7,31},{8,32},{9,... | collective-permute-start | bytes 3080 | tf_op jit(solution)/shard_map/ppermute | solution.py:15
  143.3 26.8 %collective-permute-start.12 = (bf16[8,64]{1,0:T(8,128)(2,1)S(1)}, bf16[8,64]{1,0:T(8,128)(2,1)S(1)}, u32[]{:S(2)}, u32[]{:S(2)}) collective-permute-start(bf16[8,64]{1,0:T(8,128)(2,1)S(1)} %fusion.27), channel_id=1, source_target_pairs={{0,3},{1,4},{2,5},{3,6},{4,7},{5,8},{6,9},{7,10},{8,11},{9,12},{10... | collective-permute-start | bytes 3080 | tf_op jit(solution)/shard_map/ppermute | solution.py:15
  170.1 5.3 %collective-permute-start.4 = (bf16[3,40,128]{2,0,1:T(4,128)(2,1)}, bf16[3,40,128]{2,0,1:T(4,128)(2,1)S(1)}, u32[]{:S(2)}, u32[]{:S(2)}) collective-permute-start(bf16[3,40,128]{2,0,1:T(4,128)(2,1)} %bitcast.171), channel_id=1, source_target_pairs={{0,2},{1,3},{2,4},{3,5},{4,6},{5,7},{6,8},{7,9},{8,10},{9,11},{10,... | collective-permute-start | bytes 92168 | tf_op jit(solution)/shard_map/ppermute | solution.py:15
  175.4 17.1 %collective-permute-start.5 = (bf16[3,40,128]{2,0,1:T(4,128)(2,1)}, bf16[3,40,128]{2,0,1:T(4,128)(2,1)S(1)}, u32[]{:S(2)}, u32[]{:S(2)}) collective-permute-start(bf16[3,40,128]{2,0,1:T(4,128)(2,1)} %bitcast.172), channel_id=1, source_target_pairs={{0,1},{1,2},{2,3},{3,4},{4,5},{5,6},{6,7},{7,8},{8,9},{9,10},{10,1... | collective-permute-start | bytes 92168 | tf_op jit(solution)/shard_map/ppermute | solution.py:15
  192.4 11.2 %collective-permute-start.6 = (bf16[3,40,128]{2,0,1:T(4,128)(2,1)S(1)}, bf16[3,40,128]{2,0,1:T(4,128)(2,1)S(1)}, u32[]{:S(2)}, u32[]{:S(2)}) collective-permute-start(bf16[3,40,128]{2,0,1:T(4,128)(2,1)S(1)} %bitcast.173), channel_id=1, source_target_pairs={{1,0},{2,1},{3,2},{4,3},{5,4},{6,5},{7,6},{8,7},{9,8},{10,9},{11,1... | collective-permute-start | bytes 92168 | tf_op jit(solution)/shard_map/ppermute | solution.py:15
  203.7 10.2 %collective-permute-start.7 = (bf16[3,40,128]{2,0,1:T(4,128)(2,1)S(1)}, bf16[3,40,128]{2,0,1:T(4,128)(2,1)S(1)}, u32[]{:S(2)}, u32[]{:S(2)}) collective-permute-start(bf16[3,40,128]{2,0,1:T(4,128)(2,1)S(1)} %bitcast.174), channel_id=1, source_target_pairs={{2,0},{3,1},{4,2},{5,3},{6,4},{7,5},{8,6},{9,7},{10,8},{11,9},{12,... | collective-permute-start | bytes 92168 | tf_op jit(solution)/shard_map/ppermute | solution.py:15
  213.8 5.2 %collective-permute-start.8 = (bf16[40,8,64]{2,1,0:T(8,128)(2,1)S(1)}, bf16[40,8,64]{2,1,0:T(8,128)(2,1)S(1)}, u32[]{:S(2)}, u32[]{:S(2)}) collective-permute-start(bf16[40,8,64]{2,1,0:T(8,128)(2,1)S(1)} %convolution_convert_fusion), channel_id=1, source_target_pairs={{0,2},{1,3},{2,4},{3,5},{4,6},{5,7},{6,8},{7,9},{8,10},{9,11},{10,... | collective-permute-start | bytes 122888 | tf_op jit(solution)/shard_map/ppermute | solution.py:15
  219.0 5.7 %collective-permute-start.9 = (bf16[40,8,64]{2,1,0:T(8,128)(2,1)S(1)}, bf16[40,8,64]{2,1,0:T(8,128)(2,1)S(1)}, u32[]{:S(2)}, u32[]{:S(2)}) collective-permute-start(bf16[40,8,64]{2,1,0:T(8,128)(2,1)S(1)} %convolution_convert_fusion), channel_id=1, source_target_pairs={{0,1},{1,2},{2,3},{3,4},{4,5},{5,6},{6,7},{7,8},{8,9},{9,10},{10,1... | collective-permute-start | bytes 122888 | tf_op jit(solution)/shard_map/ppermute | solution.py:15
  224.7 11.8 %collective-permute-start.10 = (bf16[40,8,64]{2,1,0:T(8,128)(2,1)S(1)}, bf16[40,8,64]{2,1,0:T(8,128)(2,1)S(1)}, u32[]{:S(2)}, u32[]{:S(2)}) collective-permute-start(bf16[40,8,64]{2,1,0:T(8,128)(2,1)S(1)} %convolution_convert_fusion), channel_id=1, source_target_pairs={{1,0},{2,1},{3,2},{4,3},{5,4},{6,5},{7,6},{8,7},{9,8},{10,9},{11,1... | collective-permute-start | bytes 122888 | tf_op jit(solution)/shard_map/ppermute | solution.py:15
  236.5 10.6 %collective-permute-start.11 = (bf16[40,8,64]{2,1,0:T(8,128)(2,1)S(1)}, bf16[40,8,64]{2,1,0:T(8,128)(2,1)S(1)}, u32[]{:S(2)}, u32[]{:S(2)}) collective-permute-start(bf16[40,8,64]{2,1,0:T(8,128)(2,1)S(1)} %convolution_convert_fusion), channel_id=1, source_target_pairs={{2,0},{3,1},{4,2},{5,3},{6,4},{7,5},{8,6},{9,7},{10,8},{11,9},{12,... | collective-permute-start | bytes 122888 | tf_op jit(solution)/shard_map/ppermute | solution.py:15
  (4 other events, 25.4 us)
where the time goes:
time: 416 us; the launch traced here: 413 us
  matrix products  121 us (29%)
  waiting for transfers between devices  117 us (28%)
  starting transfers between devices  110 us (26%)
  local copies, waits for them, and re-layouts  37.6 us (9%)
  other arithmetic  25.6 us (6%)
    ppermute x28, waiting for transfers between devices, shifted(): lax.ppermute(value, axis, [(source, source + steps) for source in range(i...  112 us
    ppermute x28, starting transfers between devices, shifted(): lax.ppermute(value, axis, [(source, source + steps) for source in range(i...  104 us
    dot_general x27, matrix products, one_slot(): jnp.einsum('lpq,alq->alp', block, sources, preferred_element_type=jnp.flo...  101 us
    reduce_and x27, other arithmetic, one_slot(): sources = jnp.take(rhs_win, chosen, axis=1)  19.1 us
    gather x27, local copies, waits for them, and re-layouts, one_slot(): others = jnp.take(coord_win, chosen, axis=1)  16.9 us
    gather x27, local copies, waits for them, and re-layouts, one_slot(): sources = jnp.take(rhs_win, chosen, axis=1)  16.3 us
    dot_general x16, matrix products, per_device(): jnp.dot(box_coef, upper_coupling[0, level, number], preferred_element_typ...  13.5 us
  transfers between devices with their start and end apart: 31, of which 25 were waited for; matrix products, arithmetic and copies ran while one was open for 6% of the time, Pallas kernels for 0%

commit v1 on v0

v1 whole, which is shorter than its diff:
```python
import functools
import math

import jax
import jax.numpy as jnp
from jax import lax
from jax.experimental import pallas as pl
from jax.experimental.pallas import tpu as pltpu
from jax.sharding import PartitionSpec as P

S_RATE = 3.0**0.5 / 0.2
C_RATE = S_RATE * math.log2(math.e)
NOISE = 0.1
OFFSETS = (-3, -2, 2, 3)
HALO = (-2, -1, 1, 2)
LEAVES = 40
PAIRS = LEAVES // 2
SLOTS = 27
LEVELS = 4
BATCH = 4
TINY = 1e-12
MESH = pl.DeviceIdType.MESH
bf16 = jnp.bfloat16
f32 = jnp.float32
NT = (((1,), (1,)), ((), ()))


def rounded(x):
    return x.astype(bf16).astype(f32)


def dot(a, b):
    return jnp.dot(a, b, preferred_element_type=f32)


def dot_nt(a, b):
    return lax.dot_general(a, b, NT, preferred_element_type=f32)


def norm_pieces(c):
    sq = c * c
    n2 = sq[0:1] + sq[1:2] + sq[2:3]
    high = rounded(n2)
    mid = rounded(n2 - high)
    low = n2 - high - mid
    return high, mid, low


def comm_kernel(
    coords,
    rhs,
    basis,
    transfer,
    up_t,
    up_c,
    win,
    cwin,
    pts,
    local,
    tsend,
    trecv,
    lev,
    lrecv,
    halo_send,
    halo_recv,
    chalo_send,
    chalo_recv,
    term_send,
    term_recv,
    lev_send,
    lev_recv,
):
    n = lax.axis_size("leaf")
    me = lax.axis_index("leaf")

    def away(k):
        return lax.rem(me + k + n, n)

    def partner(m):
        bits = [lax.rem(me, 2), lax.rem(me // 2, 2), lax.rem(me // 4, 2)]
        other = me
        for b in range(3):
            if m >> b & 1:
                other = other + (1 - 2 * bits[b]) * (1 << b)
        return other

    steps = sorted({abs(k) for k in HALO} | {abs(o) << j for j in range(LEVELS) for o in OFFSETS})
    barrier = pltpu.get_barrier_semaphore()
    greeted = [away(s) for s in steps] + [away(-s) for s in steps] + [partner(m) for m in range(1, 8)]
    for other in greeted:
        pl.semaphore_signal(barrier, inc=1, device_id=(other,), device_id_type=MESH)

    ones2 = jnp.ones((2, 128), f32)
    ones3 = jnp.ones((3, 128), f32)
    zero8 = jnp.zeros((8, 128), f32)

    def build(i, carry):
        at = pl.ds(pl.multiple_of(i * 128, 128), 128)
        c = coords[:, at].astype(f32)
        high, mid, low = norm_pieces(c)
        tile = jnp.concatenate([rhs[:, at], c, high, mid, low, ones2], axis=0)
        win[2 * LEAVES + i] = tile.astype(bf16)
        return carry

    lax.fori_loop(0, LEAVES, build, 0, unroll=4)
    pl.semaphore_wait(barrier, len(greeted))

    copies = []
    own = win.at[pl.ds(2 * LEAVES, LEAVES)]
    for num, k in enumerate(HALO):
        copies.append(
            pltpu.make_async_remote_copy(
                src_ref=own,
                dst_ref=win.at[pl.ds((2 - k) * LEAVES, LEAVES)],
                send_sem=halo_send.at[num],
                recv_sem=halo_recv.at[num],
                device_id=(away(k),),
                device_id_type=MESH,
            )
        )
        copies[-1].start()

    lane = lax.broadcasted_iota(jnp.int32, (8, 128), 1)

    def coef_four(u, total):
        halves = []
        for h in range(2):
            t = 2 * u + h
            at = pl.ds(pl.multiple_of(t * 256, 256), 256)
            r = rhs[:, at]
            both = jnp.concatenate([r[:, :128], r[:, 128:]], axis=0).astype(bf16)
            x = dot_nt(both, basis[t])
            pair = jnp.where(lane < 64, x[:8], x[8:])
            halves.append(pair)
            total = total + dot(pair.astype(bf16), transfer[t])
        cwin[PAIRS + u] = jnp.concatenate(halves, axis=0).astype(bf16)
        return total

    level_zero = lax.fori_loop(0, PAIRS // 2, coef_four, jnp.zeros((8, 64), f32), unroll=2)
    zero64 = jnp.zeros((8, 64), f32)

    def widen(x):
        return jnp.concatenate([x, zero64], axis=1)

    half = level_zero.astype(bf16)
    lev[0] = widen(half.astype(f32))
    for j in range(3):
        tsend[2 - j] = widen(dot(half, up_t[j]))

    terms = []
    for m in range(1, 8):
        count = 3 if m == 1 else 2 if m < 4 else 1
        terms.append(
            pltpu.make_async_remote_copy(
                src_ref=tsend.at[pl.ds(0, count)],
                dst_ref=trecv.at[m, pl.ds(0, count)],
                send_sem=term_send.at[m],
                recv_sem=term_recv.at[m],
                device_id=(partner(m),),
                device_id_type=MESH,
            )
        )
        terms[-1].start()

    def send_level(j):
        for num, o in enumerate(OFFSETS):
            copy = pltpu.make_async_remote_copy(
                src_ref=lev.at[j],
                dst_ref=lrecv.at[j, num],
                send_sem=lev_send.at[j, num],
                recv_sem=lev_recv.at[j, num],
                device_id=(away(-o * 2**j),),
                device_id_type=MESH,
            )
            copy.start()
            level_copies.append(copy)

    level_copies = []
    send_level(0)
    own_coef = cwin.at[pl.ds(PAIRS, PAIRS // 2)]
    for num, k in enumerate(HALO):
        copies.append(
            pltpu.make_async_remote_copy(
                src_ref=own_coef,
                dst_ref=cwin.at[pl.ds((2 - k) * (PAIRS // 2), PAIRS // 2)],
                send_sem=chalo_send.at[num],
                recv_sem=chalo_recv.at[num],
                device_id=(away(k),),
                device_id_type=MESH,
            )
        )
        copies[-1].start()

    for copy in terms:
        copy.wait()
    for j in (1, 2, 3):
        total = tsend[3 - j]
        for m in range(1, 2**j):
            total = total + trecv[m, 3 - j]
        lev[j] = rounded(total)
        send_level(j)

    def build_points(i, carry):
        at = pl.ds(pl.multiple_of(i * 128, 128), 128)
        c = coords[:, at].astype(f32)
        high, mid, low = norm_pieces(c)
        tile = jnp.concatenate([zero8, -2.0 * c, ones3, high, mid], axis=0)
        pts[i] = tile.T.astype(bf16)
        return carry

    lax.fori_loop(0, LEAVES, build_points, 0, unroll=4)

    for copy in level_copies:
        copy.wait()
    total = jnp.zeros((8, 64), f32)
    for j in range(LEVELS):
        for num, o in enumerate(OFFSETS):
            box = me // 2**j + o
            live = jnp.logical_and(box >= 0, box < n // 2**j)
            coef = lrecv[j, num][:, :64] * jnp.where(live, 1.0, 0.0)
            total = total + dot(coef.astype(bf16), up_c[4 * j + num])
    local[...] = total

    for copy in copies:
        copy.wait()
    for k in HALO:
        @pl.when(jnp.logical_or(me + k < 0, me + k >= n))
        def _(k=k):
            def clear(i, carry):
                win[(2 + k) * LEAVES + i] = jnp.zeros((16, 128), bf16)
                return carry

            def clear_coef(i, carry):
                cwin[(2 + k) * (PAIRS // 2) + i] = jnp.zeros((16, 128), bf16)
                return carry

            lax.fori_loop(0, LEAVES, clear, 0)
            lax.fori_loop(0, PAIRS // 2, clear_coef, 0)


def matern(u):
    u = jnp.maximum(u, TINY)
    r = u * lax.rsqrt(u)
    return ((1.0 + S_RATE * r) * jnp.exp2(-C_RATE * r)).astype(bf16)


def field_kernel(
    lists,
    counts,
    fars,
    win,
    cwin,
    pts,
    local,
    coupling,
    transfer,
    basis,
    rhs,
    out,
    table,
    *bufs,
):
    lane = lax.broadcasted_iota(jnp.int32, (8, 128), 1)
    first = lane < 64

    def expand(t, carry):
        x = cwin[t].astype(f32)
        y = pltpu.roll(x, 64, 1)
        for h in range(2):
            a, b = x[8 * h : 8 * h + 8], y[8 * h : 8 * h + 8]
            table[4 * t + 2 * h] = jnp.where(first, a, b)
            table[4 * t + 2 * h + 1] = jnp.where(first, b, a)
        return carry

    lax.fori_loop(0, 5 * PAIRS // 2, expand, 0, unroll=2)
    local_half = local[...].astype(bf16)

    def far_pair(t, carry):
        sums = []
        for h in range(2):
            i = 2 * t + h
            cols = [
                jnp.where(first, table[fars[i, 2 * m]], table[fars[i, 2 * m + 1]]) for m in range(4)
            ]
            x = jnp.concatenate(cols, axis=1).astype(bf16)
            sums.append(dot(x, coupling[i]))
        both = jnp.concatenate(sums, axis=1) + dot_nt(local_half, transfer[t])
        both = rounded(both)
        zero = jnp.zeros_like(both)
        split = jnp.concatenate([jnp.where(first, both, zero), jnp.where(first, zero, both)], axis=0)
        far = dot(split.astype(bf16), basis[t])
        for h in range(2):
            at = pl.ds(pl.multiple_of(t * 256 + h * 128, 128), 128)
            out[:, at] = far[8 * h : 8 * h + 8] + NOISE * rhs[:, at]
        return carry

    lax.fori_loop(0, PAIRS, far_pair, 0, unroll=2)

    def advance(leaf, s):
        n = counts[jnp.minimum(leaf, LEAVES - 1)]
        last = s + 2 >= n
        return jnp.where(last, leaf + 1, leaf), jnp.where(last, 0, s + 2)

    def batch_from(leaf, s):
        batch = []
        for _ in range(BATCH):
            batch.append((leaf, s))
            leaf, s = advance(leaf, s)
        return batch, leaf, s

    def entries(leaf, s):
        i = jnp.minimum(leaf, LEAVES - 1)
        return i, lists[i, s], lists[i, jnp.minimum(s + 1, SLOTS - 1)]

    def distances(batch, refs):
        for (leaf, s), ref in zip(batch, refs):
            i, a, b = entries(leaf, s)
            q = jnp.concatenate([win[a], win[b]], axis=1)
            ref[...] = dot(pts[i], q)

    def products(batch, refs):
        for (leaf, s), ref in zip(batch, refs):
            i, a, b = entries(leaf, s)
            live = leaf < LEAVES
            both = jnp.logical_and(live, s + 1 < counts[i])
            ra = jnp.where(live, win[a], jnp.zeros((16, 128), bf16))
            rb = jnp.where(both, win[b], jnp.zeros((16, 128), bf16))
            r = jnp.concatenate([ra, rb], axis=1)
            d = dot_nt(r, matern(ref[...]))
            at = pl.ds(pl.multiple_of(i * 128, 128), 128)
            out[:, at] += d[:8]

    tasks = lax.fori_loop(0, LEAVES, lambda i, t: t + (counts[i] + 1) // 2, jnp.int32(0))
    even, odd = bufs[:BATCH], bufs[BATCH:]
    zero = jnp.int32(0)
    batch, leaf, s = batch_from(zero, zero)
    distances(batch, even)

    def body(_, carry):
        first_leaf, first_s = carry
        now, leaf, s = batch_from(first_leaf, first_s)
        later, leaf2, s2 = batch_from(leaf, s)
        distances(later, odd)
        products(now, even)
        after, _, _ = batch_from(leaf2, s2)
        distances(after, even)
        products(later, odd)
        return leaf2, s2

    rounds = (tasks + 2 * BATCH - 1) // (2 * BATCH)
    lax.fori_loop(0, rounds, body, (zero, zero))


def run_field(lists, counts, fars, *arrays):
    smem = pl.BlockSpec(memory_space=pltpu.SMEM)
    vmem = pl.BlockSpec(memory_space=pltpu.VMEM)
    return pl.pallas_call(
        field_kernel,
        out_shape=jax.ShapeDtypeStruct((8, LEAVES * 128), f32),
        in_specs=[smem] * 3 + [vmem] * len(arrays),
        out_specs=vmem,
        scratch_shapes=[pltpu.VMEM((5 * LEAVES, 8, 128), f32)]
        + [pltpu.VMEM((128, 256), f32)] * (2 * BATCH),
        compiler_params=pltpu.CompilerParams(vmem_limit_bytes=40 * 2**20),
    )(lists, counts, fars, *arrays)


def run_comm(*arrays):
    vmem = pl.BlockSpec(memory_space=pltpu.VMEM)
    dma = pltpu.SemaphoreType.DMA
    return pl.pallas_call(
        comm_kernel,
        out_shape=[
            jax.ShapeDtypeStruct((5 * LEAVES, 16, 128), bf16),
            jax.ShapeDtypeStruct((5 * PAIRS // 2, 16, 128), bf16),
            jax.ShapeDtypeStruct((LEAVES, 128, 16), bf16),
            jax.ShapeDtypeStruct((8, 64), f32),
        ],
        in_specs=[vmem] * len(arrays),
        out_specs=[vmem] * 4,
        scratch_shapes=[
            pltpu.VMEM((3, 8, 128), f32),
            pltpu.VMEM((8, 3, 8, 128), f32),
            pltpu.VMEM((LEVELS, 8, 128), f32),
            pltpu.VMEM((LEVELS, 4, 8, 128), f32),
            dma((4,)),
            dma((4,)),
            dma((4,)),
            dma((4,)),
            dma((8,)),
            dma((8,)),
            dma((LEVELS, 4)),
            dma((LEVELS, 4)),
        ],
        compiler_params=pltpu.CompilerParams(
            collective_id=0, has_side_effects=True, vmem_limit_bytes=40 * 2**20
        ),
    )(*arrays)


def per_device(
    coords,
    rhs,
    leaf_basis,
    leaf_transfer,
    upper_transfer,
    upper_coupling,
    leaf_coupling,
    near_lists,
    near_counts,
    far_lists,
):
    basis = leaf_basis.reshape(PAIRS, 128, 128)
    transfer = leaf_transfer.reshape(PAIRS, 128, 64)
    coupling = leaf_coupling.reshape(LEAVES, 512, 64)
    win, cwin, pts, local = run_comm(
        coords, rhs, basis, transfer, upper_transfer[0], upper_coupling.reshape(16, 64, 64)
    )
    return run_field(
        near_lists, near_counts, far_lists, win, cwin, pts, local, coupling, transfer, basis, rhs
    )


def solution(mesh):
    return jax.shard_map(
        per_device,
        mesh=mesh,
        in_specs=(
            P(None, "leaf"),
            P(None, "leaf"),
            P("leaf", None, None),
            P("leaf", None, None),
            P("leaf", None, None, None),
            P("leaf", None, None, None, None),
            P("leaf", None, None, None),
            P("leaf", None),
            P("leaf"),
            P("leaf", None),
        ),
        out_specs=P(None, "leaf"),
        check_vma=False,
    )
```

time: 416 us -> 71.5 us (0.17)
  the two profiles are of different devices: /device:TPU:255 before, /device:TPU:18 now
where the time goes in v1:
time: 71.5 us; the launch traced here: 70.9 us
  Pallas kernels  57.5 us (80%)
  local copies, waits for them, and re-layouts  13.4 us (19%)
    pallas_call x1, Pallas kernels, run_field(): pl.pallas_call(field_kernel, out_shape=jax.ShapeDtypeStruct((8, LEAVES *...  28.9 us
    pallas_call x1, Pallas kernels, run_comm(): pl.pallas_call(comm_kernel, out_shape=[jax.ShapeDtypeStruct((5 * LEAVES,...  28.5 us
    unnamed x24, local copies, waits for them, and re-layouts  13.4 us

profile of v1, /device:TPU:18, one launch (start us, length us, event | category | flops | bytes accessed | tf_op | source)
XLA Modules:
  0.0 70.9 jit_solution(7111221621704379840)
XLA Ops:
  0.0 0.8 %copy.11.lists = s32[40,27]{1,0:T(8,128)S(1)} copy(s32[40,27]{0,1:T(8,128)} %param.17) | data formatting | bytes 8640 | tf_op args[7]
  0.8 0.8 %copy.12.fars = s32[40,8]{1,0:T(8,128)S(1)} copy(s32[40,8]{0,1:T(8,128)} %param.19) | data formatting | bytes 2560 | tf_op args[9]
  1.6 0.0 copy-start.1
  1.6 1.1 %copy-done.1 = bf16[40,64,128]{2,1,0:T(8,128)(2,1)S(1)} copy-done((bf16[40,64,128]{2,1,0:T(8,128)(2,1)S(1)}, bf16[40,64,128]{2,1,0:T(8,128)(2,1)}, u32[]{:S(2)}) %copy-start.1) | copy-done | bytes 655384
  2.6 0.0 copy-start.3
  2.6 1.1 %copy-done.3 = bf16[40,64,64]{2,1,0:T(8,128)(2,1)S(1)} copy-done((bf16[40,64,64]{2,1,0:T(8,128)(2,1)S(1)}, bf16[40,64,64]{2,1,0:T(8,128)(2,1)}, u32[]{:S(2)}) %copy-start.3) | copy-done | bytes 327704
  3.7 0.0 copy-start.5
  3.7 0.9 %copy-done.5 = f32[8,5120]{1,0:T(8,128)S(1)} copy-done((f32[8,5120]{1,0:T(8,128)S(1)}, f32[8,5120]{1,0:T(8,128)}, u32[]{:S(2)}) %copy-start.5) | copy-done | bytes 163864
  4.7 0.0 copy-start.7
  4.7 0.9 %copy-done.7 = bf16[1,4,4,64,64]{4,3,2,1,0:T(8,128)(2,1)S(1)} copy-done((bf16[1,4,4,64,64]{4,3,2,1,0:T(8,128)(2,1)S(1)}, bf16[1,4,4,64,64]{4,3,2,1,0:T(8,128)(2,1)}, u32[]{:S(2)}) %copy-start.7) | copy-done | bytes 131096
  5.6 0.0 copy-start.8
  5.6 0.8 %copy-done.8 = bf16[1,3,64,64]{3,2,1,0:T(8,128)(2,1)S(1)} copy-done((bf16[1,3,64,64]{3,2,1,0:T(8,128)(2,1)S(1)}, bf16[1,3,64,64]{3,2,1,0:T(8,128)(2,1)}, u32[]{:S(2)}) %copy-start.8) | copy-done | bytes 24600
  6.4 0.0 copy-start.9
  6.4 0.8 %copy-done.9 = bf16[3,5120]{1,0:T(4,128)(2,1)S(1)} copy-done((bf16[3,5120]{1,0:T(4,128)(2,1)S(1)}, bf16[3,5120]{1,0:T(4,128)(2,1)}, u32[]{:S(2)}) %copy-start.9) | copy-done | bytes 30744
  7.2 28.5 %shard_map.100 = (bf16[200,16,128]{2,1,0:T(8,128)(2,1)S(1)}, bf16[50,16,128]{2,1,0:T(8,128)(2,1)S(1)}, bf16[40,128,16]{2,1,0:T(8,128)(2,1)S(1)}, f32[8,64]{1,0:T(8,128)S(1)}) custom-call(bf16[3,5120]{1,0:T(4,128)(2,1)S(1)} %copy-done.9, f32[8,5120]{1,0:T(8,128)S(1)} %copy-done.5, bf16[20,128,128]{2,1,0:T(8,128)(2,1)S(1)} %bitcast.6, ...), custom_call_target="tpu_custom_call" | custom-call | tf_op jit(solution)/shard_map/pallas_call | solution.py:371
  35.7 0.0 copy-start
  35.7 2.5 %copy-done = bf16[40,8,64,64]{3,2,1,0:T(8,128)(2,1)S(1)} copy-done((bf16[40,8,64,64]{3,2,1,0:T(8,128)(2,1)S(1)}, bf16[40,8,64,64]{3,2,1,0:T(8,128)(2,1)}, u32[]{:S(2)}) %copy-start) | copy-done | bytes 2621464
  38.2 0.0 copy-start.2
  38.2 1.1 %copy-done.2 = bf16[40,64,128]{2,1,0:T(8,128)(2,1)S(1)} copy-done((bf16[40,64,128]{2,1,0:T(8,128)(2,1)S(1)}, bf16[40,64,128]{2,1,0:T(8,128)(2,1)}, u32[]{:S(2)}) %copy-start.2) | copy-done | bytes 655384
  39.3 0.0 copy-start.4
  39.3 1.1 %copy-done.4 = bf16[40,64,64]{2,1,0:T(8,128)(2,1)S(1)} copy-done((bf16[40,64,64]{2,1,0:T(8,128)(2,1)S(1)}, bf16[40,64,64]{2,1,0:T(8,128)(2,1)}, u32[]{:S(2)}) %copy-start.4) | copy-done | bytes 327704
  40.4 0.0 copy-start.6
  40.4 0.9 %copy-done.6 = f32[8,5120]{1,0:T(8,128)S(1)} copy-done((f32[8,5120]{1,0:T(8,128)S(1)}, f32[8,5120]{1,0:T(8,128)}, u32[]{:S(2)}) %copy-start.6) | copy-done | bytes 163864
  41.3 0.0 copy-start.10
  41.3 0.7 copy-done.10
  42.0 28.9 %shard_map.101 = f32[8,5120]{1,0:T(8,128)} custom-call(s32[40,27]{1,0:T(8,128)S(1)} %copy.11.lists, s32[40]{0:T(128)S(1)} %copy-done.10, s32[40,8]{1,0:T(8,128)S(1)} %copy.12.fars, bf16[200,16,128]{2,1,0:T(8,128)(2,1)S(1)} %get-tuple-element.9.win, bf16[50,16,128]{2,1,0:T(8,128)(2,1)S(1)} %get-tuple-element.10.cwin, ...), custom_call_target="tpu_custom_call" | custom-call | tf_op jit(solution)/shard_map/pallas_call | solution.py:357
Async XLA Ops:
  1.6 1.1 %copy-start.1 = (bf16[40,64,128]{2,1,0:T(8,128)(2,1)S(1)}, bf16[40,64,128]{2,1,0:T(8,128)(2,1)}, u32[]{:S(2)}) copy-start(bf16[40,64,128]{2,1,0:T(8,128)(2,1)} %param.12) | copy-start | bytes 1966084
  2.6 1.1 %copy-start.3 = (bf16[40,64,64]{2,1,0:T(8,128)(2,1)S(1)}, bf16[40,64,64]{2,1,0:T(8,128)(2,1)}, u32[]{:S(2)}) copy-start(bf16[40,64,64]{2,1,0:T(8,128)(2,1)} %param.13) | copy-start | bytes 983044
  3.7 0.9 %copy-start.5 = (f32[8,5120]{1,0:T(8,128)S(1)}, f32[8,5120]{1,0:T(8,128)}, u32[]{:S(2)}) copy-start(f32[8,5120]{1,0:T(8,128)} %rhs.3) | copy-start | bytes 491524
  4.7 0.9 %copy-start.7 = (bf16[1,4,4,64,64]{4,3,2,1,0:T(8,128)(2,1)S(1)}, bf16[1,4,4,64,64]{4,3,2,1,0:T(8,128)(2,1)}, u32[]{:S(2)}) copy-start(bf16[1,4,4,64,64]{4,3,2,1,0:T(8,128)(2,1)} %param.15) | copy-start | bytes 393220
  5.6 0.8 %copy-start.8 = (bf16[1,3,64,64]{3,2,1,0:T(8,128)(2,1)S(1)}, bf16[1,3,64,64]{3,2,1,0:T(8,128)(2,1)}, u32[]{:S(2)}) copy-start(bf16[1,3,64,64]{3,2,1,0:T(8,128)(2,1)} %param.14) | copy-start | bytes 73732
  6.4 0.8 %copy-start.9 = (bf16[3,5120]{1,0:T(4,128)(2,1)S(1)}, bf16[3,5120]{1,0:T(4,128)(2,1)}, u32[]{:S(2)}) copy-start(bf16[3,5120]{1,0:T(4,128)(2,1)} %coords.1) | copy-start | bytes 92164
  35.7 2.5 %copy-start = (bf16[40,8,64,64]{3,2,1,0:T(8,128)(2,1)S(1)}, bf16[40,8,64,64]{3,2,1,0:T(8,128)(2,1)}, u32[]{:S(2)}) copy-start(bf16[40,8,64,64]{3,2,1,0:T(8,128)(2,1)} %param.16) | copy-start | bytes 7864324
  38.2 1.1 %copy-start.2 = (bf16[40,64,128]{2,1,0:T(8,128)(2,1)S(1)}, bf16[40,64,128]{2,1,0:T(8,128)(2,1)}, u32[]{:S(2)}) copy-start(bf16[40,64,128]{2,1,0:T(8,128)(2,1)} %param.12) | copy-start | bytes 1966084
  39.3 1.1 %copy-start.4 = (bf16[40,64,64]{2,1,0:T(8,128)(2,1)S(1)}, bf16[40,64,64]{2,1,0:T(8,128)(2,1)}, u32[]{:S(2)}) copy-start(bf16[40,64,64]{2,1,0:T(8,128)(2,1)} %param.13) | copy-start | bytes 983044
  40.4 0.9 %copy-start.6 = (f32[8,5120]{1,0:T(8,128)S(1)}, f32[8,5120]{1,0:T(8,128)}, u32[]{:S(2)}) copy-start(f32[8,5120]{1,0:T(8,128)} %rhs.3) | copy-start | bytes 491524
  41.3 0.7 copy-start.10

commit v2 on v1

--- a/solution.py
+++ b/solution.py
@@ -17,12 +17,15 @@
 PAIRS = LEAVES // 2
 SLOTS = 27
 LEVELS = 4
-BATCH = 4
+BATCH = 8
+SIDE = 0
+FAR_UNROLL = 4
 TINY = 1e-12
 MESH = pl.DeviceIdType.MESH
 bf16 = jnp.bfloat16
 f32 = jnp.float32
 NT = (((1,), (1,)), ((), ()))
+TN = (((0,), (0,)), ((), ()))
 
 
 def rounded(x):
@@ -47,16 +50,23 @@
 
 
 def comm_kernel(
+    coords_h,
+    rhs_h,
+    basis_h,
+    transfer_h,
+    up_t_h,
+    up_c_h,
+    win,
+    cwin,
+    pts,
+    local,
     coords,
     rhs,
     basis,
     transfer,
     up_t,
     up_c,
-    win,
-    cwin,
-    pts,
-    local,
+    load_sems,
     tsend,
     trecv,
     lev,
@@ -72,6 +82,17 @@
 ):
     n = lax.axis_size("leaf")
     me = lax.axis_index("leaf")
+    pairs = [
+        (coords_h, coords),
+        (rhs_h, rhs),
+        (basis_h, basis),
+        (transfer_h, transfer),
+        (up_t_h, up_t),
+        (up_c_h, up_c),
+    ]
+    loads = [pltpu.make_async_copy(a, b, load_sems.at[num]) for num, (a, b) in enumerate(pairs)]
+    for load in loads:
+        load.start()
 
     def away(k):
         return lax.rem(me + k + n, n)
@@ -102,6 +123,8 @@
         win[2 * LEAVES + i] = tile.astype(bf16)
         return carry
 
+    for load in loads[:2]:
+        load.wait()
     lax.fori_loop(0, LEAVES, build, 0, unroll=4)
     pl.semaphore_wait(barrier, len(greeted))
 
@@ -136,6 +159,8 @@
         cwin[PAIRS + u] = jnp.concatenate(halves, axis=0).astype(bf16)
         return total
 
+    for load in loads[2:]:
+        load.wait()
     level_zero = lax.fori_loop(0, PAIRS // 2, coef_four, jnp.zeros((8, 64), f32), unroll=2)
     zero64 = jnp.zeros((8, 64), f32)
 
@@ -244,25 +269,7 @@
     return ((1.0 + S_RATE * r) * jnp.exp2(-C_RATE * r)).astype(bf16)
 
 
-def field_kernel(
-    lists,
-    counts,
-    fars,
-    win,
-    cwin,
-    pts,
-    local,
-    coupling,
-    transfer,
-    basis,
-    rhs,
-    out,
-    table,
-    *bufs,
-):
-    lane = lax.broadcasted_iota(jnp.int32, (8, 128), 1)
-    first = lane < 64
-
+def expand_coefs(cwin, table, first):
     def expand(t, carry):
         x = cwin[t].astype(f32)
         y = pltpu.roll(x, 64, 1)
@@ -272,7 +279,12 @@
             table[4 * t + 2 * h + 1] = jnp.where(first, b, a)
         return carry
 
-    lax.fori_loop(0, 5 * PAIRS // 2, expand, 0, unroll=2)
+    lax.fori_loop(0, 5 * PAIRS // 2, expand, 0, unroll=5)
+
+
+def far_phase(fars, cwin, local, coupling, transfer, basis, rhs, out, table):
+    first = lax.broadcasted_iota(jnp.int32, (8, 128), 1) < 64
+    expand_coefs(cwin, table, first)
     local_half = local[...].astype(bf16)
 
     def far_pair(t, carry):
@@ -280,7 +292,7 @@
         for h in range(2):
             i = 2 * t + h
             cols = [
-                jnp.where(first, table[fars[i, 2 * m]], table[fars[i, 2 * m + 1]]) for m in range(4)
+                jnp.where(first, table[fars[2 * m, i]], table[fars[2 * m + 1, i]]) for m in range(4)
             ]
             x = jnp.concatenate(cols, axis=1).astype(bf16)
             sums.append(dot(x, coupling[i]))
@@ -291,10 +303,15 @@
         far = dot(split.astype(bf16), basis[t])
         for h in range(2):
             at = pl.ds(pl.multiple_of(t * 256 + h * 128, 128), 128)
-            out[:, at] = far[8 * h : 8 * h + 8] + NOISE * rhs[:, at]
+            out[:, at] += far[8 * h : 8 * h + 8] + NOISE * rhs[:, at]
         return carry
 
-    lax.fori_loop(0, PAIRS, far_pair, 0, unroll=2)
+    lax.fori_loop(0, PAIRS, far_pair, 0, unroll=FAR_UNROLL)
+
+
+def near_phase(lists, counts, win, pts, out, dist, block):
+    out[...] = jnp.zeros_like(out)
+    nothing = jnp.zeros((16, 128), bf16)
 
     def advance(leaf, s):
         n = counts[jnp.minimum(leaf, LEAVES - 1)]
@@ -310,63 +327,129 @@
 
     def entries(leaf, s):
         i = jnp.minimum(leaf, LEAVES - 1)
-        return i, lists[i, s], lists[i, jnp.minimum(s + 1, SLOTS - 1)]
-
-    def distances(batch, refs):
-        for (leaf, s), ref in zip(batch, refs):
-            i, a, b = entries(leaf, s)
-            q = jnp.concatenate([win[a], win[b]], axis=1)
-            ref[...] = dot(pts[i], q)
-
-    def products(batch, refs):
-        for (leaf, s), ref in zip(batch, refs):
-            i, a, b = entries(leaf, s)
-            live = leaf < LEAVES
-            both = jnp.logical_and(live, s + 1 < counts[i])
-            ra = jnp.where(live, win[a], jnp.zeros((16, 128), bf16))
-            rb = jnp.where(both, win[b], jnp.zeros((16, 128), bf16))
-            r = jnp.concatenate([ra, rb], axis=1)
-            d = dot_nt(r, matern(ref[...]))
-            at = pl.ds(pl.multiple_of(i * 128, 128), 128)
-            out[:, at] += d[:8]
+        return i, lists[s, i], lists[jnp.minimum(s + 1, SLOTS - 1), i]
+
+    def distance(leaf, s, g):
+        i, a, b = entries(leaf, s)
+        q = jnp.concatenate([win[a], win[b]], axis=1 - SIDE)
+        if SIDE:
+            dist[g] = lax.dot_general(q, pts[i], TN, preferred_element_type=f32)
+        else:
+            dist[g] = dot(pts[i], q)
+
+    def values(g):
+        block[g] = matern(dist[g])
+
+    def product(leaf, s, g):
+        i, a, b = entries(leaf, s)
+        live = leaf < LEAVES
+        both = jnp.logical_and(live, s + 1 < counts[i])
+        ra = jnp.where(live, win[a], nothing)
+        rb = jnp.where(both, win[b], nothing)
+        r = jnp.concatenate([ra, rb], axis=1)
+        k = block[g]
+        if SIDE:
+            d = dot(r, jnp.concatenate([k[:, :128], k[:, 128:]], axis=0))
+        else:
+            d = dot_nt(r, k)
+        at = pl.ds(pl.multiple_of(i * 128, 128), 128)
+        out[:, at] += d[:8]
 
     tasks = lax.fori_loop(0, LEAVES, lambda i, t: t + (counts[i] + 1) // 2, jnp.int32(0))
-    even, odd = bufs[:BATCH], bufs[BATCH:]
     zero = jnp.int32(0)
-    batch, leaf, s = batch_from(zero, zero)
-    distances(batch, even)
+    now, leaf, s = batch_from(zero, zero)
+    for g in range(BATCH):
+        distance(*now[g], g)
+    mid, leaf, s = batch_from(leaf, s)
+    for g in range(BATCH):
+        values(g)
+        distance(*mid[g], g)
 
     def body(_, carry):
-        first_leaf, first_s = carry
-        now, leaf, s = batch_from(first_leaf, first_s)
-        later, leaf2, s2 = batch_from(leaf, s)
-        distances(later, odd)
-        products(now, even)
-        after, _, _ = batch_from(leaf2, s2)
-        distances(after, even)
-        products(later, odd)
-        return leaf2, s2
-
-    rounds = (tasks + 2 * BATCH - 1) // (2 * BATCH)
-    lax.fori_loop(0, rounds, body, (zero, zero))
-
-
-def run_field(lists, counts, fars, *arrays):
-    smem = pl.BlockSpec(memory_space=pltpu.SMEM)
+        now, mid, leaf, s = carry
+        later, leaf, s = batch_from(leaf, s)
+        for g in range(BATCH):
+            product(*now[g], g)
+            values(g)
+            distance(*later[g], g)
+        return mid, later, leaf, s
+
+    lax.fori_loop(0, (tasks + BATCH - 1) // BATCH, body, (now, mid, leaf, s))
+
+
+def field_kernel(
+    lists_h,
+    counts_h,
+    fars_h,
+    coupling_h,
+    transfer_h,
+    basis_h,
+    rhs_h,
+    win,
+    cwin,
+    pts,
+    local,
+    out,
+    lists,
+    counts,
+    fars,
+    coupling,
+    transfer,
+    basis,
+    rhs,
+    sems,
+    table,
+    dist,
+    block,
+):
+    pairs = [
+        (lists_h, lists),
+        (counts_h, counts),
+        (fars_h, fars),
+        (coupling_h, coupling),
+        (transfer_h, transfer),
+        (basis_h, basis),
+        (rhs_h, rhs),
+    ]
+    copies = [pltpu.make_async_copy(a, b, sems.at[n]) for n, (a, b) in enumerate(pairs)]
+    for copy in copies:
+        copy.start()
+    for copy in copies[:2]:
+        copy.wait()
+    near_phase(lists, counts, win, pts, out, dist, block)
+    for copy in copies[2:]:
+        copy.wait()
+    far_phase(fars, cwin, local, coupling, transfer, basis, rhs, out, table)
+
+
+def run_field(lists, counts, fars, coupling, transfer, basis, rhs, *arrays):
+    hbm = pl.BlockSpec(memory_space=pltpu.HBM)
     vmem = pl.BlockSpec(memory_space=pltpu.VMEM)
     return pl.pallas_call(
         field_kernel,
         out_shape=jax.ShapeDtypeStruct((8, LEAVES * 128), f32),
-        in_specs=[smem] * 3 + [vmem] * len(arrays),
+        in_specs=[hbm] * 7 + [vmem] * len(arrays),
         out_specs=vmem,
-        scratch_shapes=[pltpu.VMEM((5 * LEAVES, 8, 128), f32)]
-        + [pltpu.VMEM((128, 256), f32)] * (2 * BATCH),
-        compiler_params=pltpu.CompilerParams(vmem_limit_bytes=40 * 2**20),
-    )(lists, counts, fars, *arrays)
+        scratch_shapes=[
+            pltpu.SMEM((SLOTS, LEAVES), jnp.int32),
+            pltpu.SMEM((LEAVES,), jnp.int32),
+            pltpu.SMEM((8, LEAVES), jnp.int32),
+            pltpu.VMEM((LEAVES, 512, 64), bf16),
+            pltpu.VMEM((PAIRS, 128, 64), bf16),
+            pltpu.VMEM((PAIRS, 128, 128), bf16),
+            pltpu.VMEM((8, LEAVES * 128), f32),
+            pltpu.SemaphoreType.DMA((7,)),
+            pltpu.VMEM((5 * LEAVES, 8, 128), f32),
+            pltpu.VMEM((BATCH, 128, 256), f32),
+            pltpu.VMEM((BATCH, 128, 256), bf16),
+        ],
+        compiler_params=pltpu.CompilerParams(vmem_limit_bytes=60 * 2**20),
+    )(lists, counts, fars, coupling, transfer, basis, rhs, *arrays)
 
 
 def run_comm(*arrays):
     vmem = pl.BlockSpec(memory_space=pltpu.VMEM)
+    hbm = pl.BlockSpec(memory_space=pltpu.HBM)
     dma = pltpu.SemaphoreType.DMA
     return pl.pallas_call(
         comm_kernel,
@@ -376,9 +459,11 @@
             jax.ShapeDtypeStruct((LEAVES, 128, 16), bf16),
             jax.ShapeDtypeStruct((8, 64), f32),
         ],
-        in_specs=[vmem] * len(arrays),
+        in_specs=[hbm] * len(arrays),
         out_specs=[vmem] * 4,
-        scratch_shapes=[
+        scratch_shapes=[pltpu.VMEM(x.shape, x.dtype) for x in arrays]
+        + [
+            dma((6,)),
             pltpu.VMEM((3, 8, 128), f32),
             pltpu.VMEM((8, 3, 8, 128), f32),
             pltpu.VMEM((LEVELS, 8, 128), f32),
@@ -393,7 +478,7 @@
             dma((LEVELS, 4)),
         ],
         compiler_params=pltpu.CompilerParams(
-            collective_id=0, has_side_effects=True, vmem_limit_bytes=40 * 2**20
+            collective_id=0, has_side_effects=True, vmem_limit_bytes=60 * 2**20
         ),
     )(*arrays)
 
@@ -417,7 +502,7 @@
         coords, rhs, basis, transfer, upper_transfer[0], upper_coupling.reshape(16, 64, 64)
     )
     return run_field(
-        near_lists, near_counts, far_lists, win, cwin, pts, local, coupling, transfer, basis, rhs
+        near_lists.T, near_counts, far_lists.T, coupling, transfer, basis, rhs, win, cwin, pts, local
     )
 
 

time: 71.5 us -> 59.4 us (0.83)
  the two profiles are of different devices: /device:TPU:18 before, /device:TPU:2 now
where the time goes in v2:
time: 59.4 us; the launch traced here: 59.2 us
  Pallas kernels  59.2 us (100%)
    pallas_call x1, Pallas kernels, run_comm(): pl.pallas_call(comm_kernel, out_shape=[jax.ShapeDtypeStruct((5 * LEAVES,...  31.8 us
    pallas_call x1, Pallas kernels, run_field(): pl.pallas_call(field_kernel, out_shape=jax.ShapeDtypeStruct((8, LEAVES *...  27.5 us

profile of v2, /device:TPU:2, one launch (start us, length us, event | category | flops | bytes accessed | tf_op | source)
XLA Modules:
  0.0 59.2 jit_solution(5564644344098728274)
XLA Ops:
  0.0 31.8 %shard_map.100 = (bf16[200,16,128]{2,1,0:T(8,128)(2,1)}, bf16[50,16,128]{2,1,0:T(8,128)(2,1)}, bf16[40,128,16]{2,1,0:T(8,128)(2,1)}, f32[8,64]{1,0:T(8,128)}) custom-call(bf16[3,5120]{1,0:T(4,128)(2,1)} %coords_h.1, f32[8,5120]{1,0:T(8,128)} %rhs_h.3, bf16[20,128,128]{2,1,0:T(8,128)(2,1)} %bitcast.10, bf16[20,128,64]{2,1,0:T(8,128)(2,1)} %bitcast.8, ...), custom_call_target="tpu_custom_call" | custom-call | tf_op jit(solution)/shard_map/pallas_call | solution.py:454
  31.8 27.5 %shard_map.101 = f32[8,5120]{1,0:T(8,128)} custom-call(s32[27,40]{1,0:T(8,128)} %bitcast.14, s32[40]{0:T(128)} %counts_h.1, s32[8,40]{1,0:T(8,128)} %bitcast.15, bf16[40,512,64]{2,1,0:T(8,128)(2,1)} %bitcast.7, bf16[20,128,64]{2,1,0:T(8,128)(2,1)} %bitcast.9, bf16[20,128,128]{2,1,0:T(8,128)(2,1)} %bitcast.11, f32[8,5120]{1,0:T(8,128)} %rhs_h.3, ...), custom_call_target="tpu_custom_call" | custom-call | tf_op jit(solution)/shard_map/pallas_call | solution.py:428

commit v3 on v2

--- a/solution.py
+++ b/solution.py
@@ -20,6 +20,7 @@
 BATCH = 8
 SIDE = 0
 FAR_UNROLL = 4
+COEF_UNROLL = 2
 TINY = 1e-12
 MESH = pl.DeviceIdType.MESH
 bf16 = jnp.bfloat16
@@ -105,11 +106,22 @@
                 other = other + (1 - 2 * bits[b]) * (1 << b)
         return other
 
+    def inside(k):
+        return jnp.logical_and(me + k >= 0, me + k < n)
+
     steps = sorted({abs(k) for k in HALO} | {abs(o) << j for j in range(LEVELS) for o in OFFSETS})
+    steps = steps + [-k for k in steps]
+    lrecv[...] = jnp.zeros_like(lrecv)
     barrier = pltpu.get_barrier_semaphore()
-    greeted = [away(s) for s in steps] + [away(-s) for s in steps] + [partner(m) for m in range(1, 8)]
-    for other in greeted:
-        pl.semaphore_signal(barrier, inc=1, device_id=(other,), device_id_type=MESH)
+    for m in range(1, 8):
+        pl.semaphore_signal(barrier, inc=1, device_id=(partner(m),), device_id_type=MESH)
+    greeted = jnp.int32(7)
+    for k in steps:
+        greeted = greeted + jnp.where(inside(k), 1, 0)
+
+        @pl.when(inside(k))
+        def _(k=k):
+            pl.semaphore_signal(barrier, inc=1, device_id=(away(k),), device_id_type=MESH)
 
     ones2 = jnp.ones((2, 128), f32)
     ones3 = jnp.ones((3, 128), f32)
@@ -126,22 +138,6 @@
     for load in loads[:2]:
         load.wait()
     lax.fori_loop(0, LEAVES, build, 0, unroll=4)
-    pl.semaphore_wait(barrier, len(greeted))
-
-    copies = []
-    own = win.at[pl.ds(2 * LEAVES, LEAVES)]
-    for num, k in enumerate(HALO):
-        copies.append(
-            pltpu.make_async_remote_copy(
-                src_ref=own,
-                dst_ref=win.at[pl.ds((2 - k) * LEAVES, LEAVES)],
-                send_sem=halo_send.at[num],
-                recv_sem=halo_recv.at[num],
-                device_id=(away(k),),
-                device_id_type=MESH,
-            )
-        )
-        copies[-1].start()
 
     lane = lax.broadcasted_iota(jnp.int32, (8, 128), 1)
 
@@ -161,7 +157,7 @@
 
     for load in loads[2:]:
         load.wait()
-    level_zero = lax.fori_loop(0, PAIRS // 2, coef_four, jnp.zeros((8, 64), f32), unroll=2)
+    level_zero = lax.fori_loop(0, PAIRS // 2, coef_four, jnp.zeros((8, 64), f32), unroll=COEF_UNROLL)
     zero64 = jnp.zeros((8, 64), f32)
 
     def widen(x):
@@ -171,6 +167,22 @@
     lev[0] = widen(half.astype(f32))
     for j in range(3):
         tsend[2 - j] = widen(dot(half, up_t[j]))
+
+    for k in HALO:
+        @pl.when(jnp.logical_not(inside(k)))
+        def _(k=k):
+            def clear(i, carry):
+                win[(2 + k) * LEAVES + i] = jnp.zeros((16, 128), bf16)
+                return carry
+
+            def clear_coef(i, carry):
+                cwin[(2 + k) * (PAIRS // 2) + i] = jnp.zeros((16, 128), bf16)
+                return carry
+
+            lax.fori_loop(0, LEAVES, clear, 0)
+            lax.fori_loop(0, PAIRS // 2, clear_coef, 0)
+
+    pl.semaphore_wait(barrier, greeted)
 
     terms = []
     for m in range(1, 8):
@@ -187,34 +199,53 @@
         )
         terms[-1].start()
 
+    copies = []
+
+    def begin(k, copy):
+        copies.append((k, copy))
+
+        @pl.when(inside(k))
+        def _():
+            copy.start()
+
+    def finish(some):
+        for k, copy in some:
+            @pl.when(inside(k))
+            def _(copy=copy):
+                copy.wait_send()
+
+            @pl.when(inside(-k))
+            def _(copy=copy):
+                copy.wait_recv()
+
     def send_level(j):
         for num, o in enumerate(OFFSETS):
+            k = -o * 2**j
             copy = pltpu.make_async_remote_copy(
                 src_ref=lev.at[j],
                 dst_ref=lrecv.at[j, num],
                 send_sem=lev_send.at[j, num],
                 recv_sem=lev_recv.at[j, num],
-                device_id=(away(-o * 2**j),),
-                device_id_type=MESH,
-            )
-            copy.start()
-            level_copies.append(copy)
-
-    level_copies = []
-    send_level(0)
-    own_coef = cwin.at[pl.ds(PAIRS, PAIRS // 2)]
-    for num, k in enumerate(HALO):
-        copies.append(
-            pltpu.make_async_remote_copy(
-                src_ref=own_coef,
-                dst_ref=cwin.at[pl.ds((2 - k) * (PAIRS // 2), PAIRS // 2)],
-                send_sem=chalo_send.at[num],
-                recv_sem=chalo_recv.at[num],
                 device_id=(away(k),),
                 device_id_type=MESH,
             )
-        )
-        copies[-1].start()
+            begin(k, copy)
+
+    send_level(0)
+    for ref, rows, send, recv in (
+        (win, LEAVES, halo_send, halo_recv),
+        (cwin, PAIRS // 2, chalo_send, chalo_recv),
+    ):
+        for num, k in enumerate(HALO):
+            copy = pltpu.make_async_remote_copy(
+                src_ref=ref.at[pl.ds(2 * rows, rows)],
+                dst_ref=ref.at[pl.ds((2 - k) * rows, rows)],
+                send_sem=send.at[num],
+                recv_sem=recv.at[num],
+                device_id=(away(k),),
+                device_id_type=MESH,
+            )
+            begin(k, copy)
 
     for copy in terms:
         copy.wait()
@@ -235,32 +266,15 @@
 
     lax.fori_loop(0, LEAVES, build_points, 0, unroll=4)
 
-    for copy in level_copies:
-        copy.wait()
+    level_copies = copies[:4] + copies[12:]
+    finish(level_copies)
     total = jnp.zeros((8, 64), f32)
     for j in range(LEVELS):
-        for num, o in enumerate(OFFSETS):
-            box = me // 2**j + o
-            live = jnp.logical_and(box >= 0, box < n // 2**j)
-            coef = lrecv[j, num][:, :64] * jnp.where(live, 1.0, 0.0)
+        for num in range(4):
+            coef = lrecv[j, num][:, :64]
             total = total + dot(coef.astype(bf16), up_c[4 * j + num])
     local[...] = total
-
-    for copy in copies:
-        copy.wait()
-    for k in HALO:
-        @pl.when(jnp.logical_or(me + k < 0, me + k >= n))
-        def _(k=k):
-            def clear(i, carry):
-                win[(2 + k) * LEAVES + i] = jnp.zeros((16, 128), bf16)
-                return carry
-
-            def clear_coef(i, carry):
-                cwin[(2 + k) * (PAIRS // 2) + i] = jnp.zeros((16, 128), bf16)
-                return carry
-
-            lax.fori_loop(0, LEAVES, clear, 0)
-            lax.fori_loop(0, PAIRS // 2, clear_coef, 0)
+    finish(copies[4:12])
 
 
 def matern(u):

time: 59.4 us -> 51.9 us (0.87)
  the two profiles are of different devices: /device:TPU:2 before, /device:TPU:241 now
where the time goes in v3:
time: 51.9 us; the launch traced here: 51.7 us
  Pallas kernels  51.7 us (100%)
    pallas_call x1, Pallas kernels, run_field(): pl.pallas_call(field_kernel, out_shape=jax.ShapeDtypeStruct((8, LEAVES *...  28.4 us
    pallas_call x1, Pallas kernels, run_comm(): pl.pallas_call(comm_kernel, out_shape=[jax.ShapeDtypeStruct((5 * LEAVES,...  23.4 us

profile of v3, /device:TPU:241, one launch (start us, length us, event | category | flops | bytes accessed | tf_op | source)
XLA Modules:
  0.0 51.7 jit_solution(1135054001884150126)
XLA Ops:
  0.0 23.4 %shard_map.100 = (bf16[200,16,128]{2,1,0:T(8,128)(2,1)}, bf16[50,16,128]{2,1,0:T(8,128)(2,1)}, bf16[40,128,16]{2,1,0:T(8,128)(2,1)}, f32[8,64]{1,0:T(8,128)}) custom-call(bf16[3,5120]{1,0:T(4,128)(2,1)} %coords_h.1, f32[8,5120]{1,0:T(8,128)} %rhs_h.3, bf16[20,128,128]{2,1,0:T(8,128)(2,1)} %bitcast.10, bf16[20,128,64]{2,1,0:T(8,128)(2,1)} %bitcast.8, ...), custom_call_target="tpu_custom_call" | custom-call | tf_op jit(solution)/shard_map/pallas_call | solution.py:468
  23.4 28.4 %shard_map.101 = f32[8,5120]{1,0:T(8,128)} custom-call(s32[27,40]{1,0:T(8,128)} %bitcast.14, s32[40]{0:T(128)} %counts_h.1, s32[8,40]{1,0:T(8,128)} %bitcast.15, bf16[40,512,64]{2,1,0:T(8,128)(2,1)} %bitcast.7, bf16[20,128,64]{2,1,0:T(8,128)(2,1)} %bitcast.9, bf16[20,128,128]{2,1,0:T(8,128)(2,1)} %bitcast.11, f32[8,5120]{1,0:T(8,128)} %rhs_h.3, ...), custom_call_target="tpu_custom_call" | custom-call | tf_op jit(solution)/shard_map/pallas_call | solution.py:442

commit v4 on v3

--- a/solution.py
+++ b/solution.py
@@ -19,7 +19,6 @@
 LEVELS = 4
 BATCH = 8
 SIDE = 0
-FAR_UNROLL = 4
 COEF_UNROLL = 2
 TINY = 1e-12
 MESH = pl.DeviceIdType.MESH
@@ -59,8 +58,8 @@
     up_c_h,
     win,
     cwin,
-    pts,
-    local,
+    pts_h,
+    local_h,
     coords,
     rhs,
     basis,
@@ -68,6 +67,13 @@
     up_t,
     up_c,
     load_sems,
+    own,
+    cown,
+    pts,
+    local,
+    blank,
+    store_sems,
+    blank_sems,
     tsend,
     trecv,
     lev,
@@ -132,7 +138,7 @@
         c = coords[:, at].astype(f32)
         high, mid, low = norm_pieces(c)
         tile = jnp.concatenate([rhs[:, at], c, high, mid, low, ones2], axis=0)
-        win[2 * LEAVES + i] = tile.astype(bf16)
+        own[i] = tile.astype(bf16)
         return carry
 
     for load in loads[:2]:
@@ -152,7 +158,7 @@
             pair = jnp.where(lane < 64, x[:8], x[8:])
             halves.append(pair)
             total = total + dot(pair.astype(bf16), transfer[t])
-        cwin[PAIRS + u] = jnp.concatenate(halves, axis=0).astype(bf16)
+        cown[u] = jnp.concatenate(halves, axis=0).astype(bf16)
         return total
 
     for load in loads[2:]:
@@ -168,19 +174,31 @@
     for j in range(3):
         tsend[2 - j] = widen(dot(half, up_t[j]))
 
-    for k in HALO:
+    blank[...] = jnp.zeros_like(blank)
+    stores = [
+        pltpu.make_async_copy(own, win.at[pl.ds(2 * LEAVES, LEAVES)], store_sems.at[0]),
+        pltpu.make_async_copy(cown, cwin.at[pl.ds(PAIRS, PAIRS // 2)], store_sems.at[1]),
+    ]
+    for store in stores:
+        store.start()
+
+    def clears(num, k):
+        return (
+            pltpu.make_async_copy(
+                blank, win.at[pl.ds((2 + k) * LEAVES, LEAVES)], blank_sems.at[num, 0]
+            ),
+            pltpu.make_async_copy(
+                blank.at[pl.ds(0, PAIRS // 2)],
+                cwin.at[pl.ds((2 + k) * (PAIRS // 2), PAIRS // 2)],
+                blank_sems.at[num, 1],
+            ),
+        )
+
+    for num, k in enumerate(HALO):
         @pl.when(jnp.logical_not(inside(k)))
-        def _(k=k):
-            def clear(i, carry):
-                win[(2 + k) * LEAVES + i] = jnp.zeros((16, 128), bf16)
-                return carry
-
-            def clear_coef(i, carry):
-                cwin[(2 + k) * (PAIRS // 2) + i] = jnp.zeros((16, 128), bf16)
-                return carry
-
-            lax.fori_loop(0, LEAVES, clear, 0)
-            lax.fori_loop(0, PAIRS // 2, clear_coef, 0)
+        def _(num=num, k=k):
+            for clear in clears(num, k):
+                clear.start()
 
     pl.semaphore_wait(barrier, greeted)
 
@@ -232,13 +250,13 @@
             begin(k, copy)
 
     send_level(0)
-    for ref, rows, send, recv in (
-        (win, LEAVES, halo_send, halo_recv),
-        (cwin, PAIRS // 2, chalo_send, chalo_recv),
+    for mine, ref, rows, send, recv in (
+        (own, win, LEAVES, halo_send, halo_recv),
+        (cown, cwin, PAIRS // 2, chalo_send, chalo_recv),
     ):
         for num, k in enumerate(HALO):
             copy = pltpu.make_async_remote_copy(
-                src_ref=ref.at[pl.ds(2 * rows, rows)],
+                src_ref=mine,
                 dst_ref=ref.at[pl.ds((2 - k) * rows, rows)],
                 send_sem=send.at[num],
                 recv_sem=recv.at[num],
@@ -265,6 +283,8 @@
         return carry
 
     lax.fori_loop(0, LEAVES, build_points, 0, unroll=4)
+    stores.append(pltpu.make_async_copy(pts, pts_h, store_sems.at[2]))
+    stores[-1].start()
 
     level_copies = copies[:4] + copies[12:]
     finish(level_copies)
@@ -274,6 +294,16 @@
             coef = lrecv[j, num][:, :64]
             total = total + dot(coef.astype(bf16), up_c[4 * j + num])
     local[...] = total
+    stores.append(pltpu.make_async_copy(local, local_h, store_sems.at[3]))
+    stores[-1].start()
+    for store in stores:
+        store.wait()
+    for num, k in enumerate(HALO):
+        @pl.when(jnp.logical_not(inside(k)))
+        def _(num=num, k=k):
+            for clear in clears(num, k):
+                clear.wait()
+
     finish(copies[4:12])
 
 
@@ -296,12 +326,12 @@
     lax.fori_loop(0, 5 * PAIRS // 2, expand, 0, unroll=5)
 
 
-def far_phase(fars, cwin, local, coupling, transfer, basis, rhs, out, table):
+def far_stage(fars, cwin, local, coupling, transfer, basis, rhs, out, table, held):
     first = lax.broadcasted_iota(jnp.int32, (8, 128), 1) < 64
     expand_coefs(cwin, table, first)
     local_half = local[...].astype(bf16)
 
-    def far_pair(t, carry):
+    def far_sums(t):
         sums = []
         for h in range(2):
             i = 2 * t + h
@@ -311,19 +341,21 @@
             x = jnp.concatenate(cols, axis=1).astype(bf16)
             sums.append(dot(x, coupling[i]))
         both = jnp.concatenate(sums, axis=1) + dot_nt(local_half, transfer[t])
-        both = rounded(both)
+        held[...] = rounded(both)
+
+    def far_field(t):
+        both = held[...]
         zero = jnp.zeros_like(both)
         split = jnp.concatenate([jnp.where(first, both, zero), jnp.where(first, zero, both)], axis=0)
         far = dot(split.astype(bf16), basis[t])
         for h in range(2):
             at = pl.ds(pl.multiple_of(t * 256 + h * 128, 128), 128)
             out[:, at] += far[8 * h : 8 * h + 8] + NOISE * rhs[:, at]
-        return carry
-
-    lax.fori_loop(0, PAIRS, far_pair, 0, unroll=FAR_UNROLL)
-
-
-def near_phase(lists, counts, win, pts, out, dist, block):
+
+    return far_sums, far_field
+
+
+def field_phase(lists, counts, win, pts, out, dist, block, prepare_far):
     out[...] = jnp.zeros_like(out)
     nothing = jnp.zeros((16, 128), bf16)
 
@@ -379,16 +411,32 @@
         values(g)
         distance(*mid[g], g)
 
-    def body(_, carry):
+    def near_step(carry, extra=None):
         now, mid, leaf, s = carry
         later, leaf, s = batch_from(leaf, s)
         for g in range(BATCH):
+            if extra and g in extra:
+                extra[g]()
             product(*now[g], g)
             values(g)
             distance(*later[g], g)
         return mid, later, leaf, s
 
-    lax.fori_loop(0, (tasks + BATCH - 1) // BATCH, body, (now, mid, leaf, s))
+    rounds = (tasks + BATCH - 1) // BATCH
+    shared = jnp.minimum(rounds, PAIRS)
+    carry = lax.fori_loop(0, rounds - shared, lambda _, c: near_step(c), (now, mid, leaf, s))
+    far_sums, far_field = prepare_far()
+
+    def both_steps(t, carry):
+        return near_step(carry, {1: lambda: far_sums(t), 7: lambda: far_field(t)})
+
+    def far_step(t, carry):
+        far_sums(t)
+        far_field(t)
+        return carry
+
+    lax.fori_loop(0, shared, both_steps, carry)
+    lax.fori_loop(shared, PAIRS, far_step, 0)
 
 
 def field_kernel(
@@ -399,10 +447,10 @@
     transfer_h,
     basis_h,
     rhs_h,
-    win,
-    cwin,
-    pts,
-    local,
+    win_h,
+    cwin_h,
+    pts_h,
+    local_h,
     out,
     lists,
     counts,
@@ -411,29 +459,42 @@
     transfer,
     basis,
     rhs,
+    win,
+    cwin,
+    pts,
+    local,
     sems,
     table,
+    held,
     dist,
     block,
 ):
     pairs = [
         (lists_h, lists),
         (counts_h, counts),
+        (win_h, win),
+        (pts_h, pts),
         (fars_h, fars),
+        (cwin_h, cwin),
+        (local_h, local),
         (coupling_h, coupling),
         (transfer_h, transfer),
         (basis_h, basis),
         (rhs_h, rhs),
     ]
     copies = [pltpu.make_async_copy(a, b, sems.at[n]) for n, (a, b) in enumerate(pairs)]
-    for copy in copies:
+    for copy in copies[:4]:
         copy.start()
-    for copy in copies[:2]:
+    for copy in copies[:4]:
         copy.wait()
-    near_phase(lists, counts, win, pts, out, dist, block)
-    for copy in copies[2:]:
-        copy.wait()
-    far_phase(fars, cwin, local, coupling, transfer, basis, rhs, out, table)
+    for copy in copies[4:]:
+        copy.start()
+    def prepare_far():
+        for copy in copies[4:]:
+            copy.wait()
+        return far_stage(fars, cwin, local, coupling, transfer, basis, rhs, out, table, held)
+
+    field_phase(lists, counts, win, pts, out, dist, block, prepare_far)
 
 
 def run_field(lists, counts, fars, coupling, transfer, basis, rhs, *arrays):
@@ -442,7 +503,7 @@
     return pl.pallas_call(
         field_kernel,
         out_shape=jax.ShapeDtypeStruct((8, LEAVES * 128), f32),
-        in_specs=[hbm] * 7 + [vmem] * len(arrays),
+        in_specs=[hbm] * (7 + len(arrays)),
         out_specs=vmem,
         scratch_shapes=[
             pltpu.SMEM((SLOTS, LEAVES), jnp.int32),
@@ -452,8 +513,10 @@
             pltpu.VMEM((PAIRS, 128, 64), bf16),
             pltpu.VMEM((PAIRS, 128, 128), bf16),
             pltpu.VMEM((8, LEAVES * 128), f32),
-            pltpu.SemaphoreType.DMA((7,)),
+            *[pltpu.VMEM(x.shape, x.dtype) for x in arrays],
+            pltpu.SemaphoreType.DMA((11,)),
             pltpu.VMEM((5 * LEAVES, 8, 128), f32),
+            pltpu.VMEM((8, 128), f32),
             pltpu.VMEM((BATCH, 128, 256), f32),
             pltpu.VMEM((BATCH, 128, 256), bf16),
         ],
@@ -462,7 +525,6 @@
 
 
 def run_comm(*arrays):
-    vmem = pl.BlockSpec(memory_space=pltpu.VMEM)
     hbm = pl.BlockSpec(memory_space=pltpu.HBM)
     dma = pltpu.SemaphoreType.DMA
     return pl.pallas_call(
@@ -474,10 +536,17 @@
             jax.ShapeDtypeStruct((8, 64), f32),
         ],
         in_specs=[hbm] * len(arrays),
-        out_specs=[vmem] * 4,
+        out_specs=[hbm] * 4,
         scratch_shapes=[pltpu.VMEM(x.shape, x.dtype) for x in arrays]
         + [
             dma((6,)),
+            pltpu.VMEM((LEAVES, 16, 128), bf16),
+            pltpu.VMEM((PAIRS // 2, 16, 128), bf16),
+            pltpu.VMEM((LEAVES, 128, 16), bf16),
+            pltpu.VMEM((8, 64), f32),
+            pltpu.VMEM((LEAVES, 16, 128), bf16),
+            dma((4,)),
+            dma((4, 2)),
             pltpu.VMEM((3, 8, 128), f32),
             pltpu.VMEM((8, 3, 8, 128), f32),
             pltpu.VMEM((LEVELS, 8, 128), f32),

time: 51.9 us -> 45 us (0.87)
  the two profiles are of different devices: /device:TPU:241 before, /device:TPU:240 now
where the time goes in v4:
time: 45 us; the launch traced here: 44.8 us
  Pallas kernels  44.8 us (100%)
    pallas_call x1, Pallas kernels, run_field(): pl.pallas_call(field_kernel, out_shape=jax.ShapeDtypeStruct((8, LEAVES *...  22.5 us
    pallas_call x1, Pallas kernels, run_comm(): pl.pallas_call(comm_kernel, out_shape=[jax.ShapeDtypeStruct((5 * LEAVES,...  22.4 us

profile of v4, /device:TPU:240, one launch (start us, length us, event | category | flops | bytes accessed | tf_op | source)
XLA Modules:
  0.0 44.8 jit_solution(11690198694385587236)
XLA Ops:
  0.0 22.4 %shard_map.100 = (bf16[200,16,128]{2,1,0:T(8,128)(2,1)}, bf16[50,16,128]{2,1,0:T(8,128)(2,1)}, bf16[40,128,16]{2,1,0:T(8,128)(2,1)}, f32[8,64]{1,0:T(8,128)}) custom-call(bf16[3,5120]{1,0:T(4,128)(2,1)} %coords_h.1, f32[8,5120]{1,0:T(8,128)} %rhs_h.3, bf16[20,128,128]{2,1,0:T(8,128)(2,1)} %bitcast.10, bf16[20,128,64]{2,1,0:T(8,128)(2,1)} %bitcast.8, ...), custom_call_target="tpu_custom_call" | custom-call | tf_op jit(solution)/shard_map/pallas_call | solution.py:530
  22.4 22.5 %shard_map.101 = f32[8,5120]{1,0:T(8,128)} custom-call(s32[27,40]{1,0:T(8,128)} %bitcast.14, s32[40]{0:T(128)} %counts_h.1, s32[8,40]{1,0:T(8,128)} %bitcast.15, bf16[40,512,64]{2,1,0:T(8,128)(2,1)} %bitcast.7, bf16[20,128,64]{2,1,0:T(8,128)(2,1)} %bitcast.9, bf16[20,128,128]{2,1,0:T(8,128)(2,1)} %bitcast.11, f32[8,5120]{1,0:T(8,128)} %rhs_h.3, ...), custom_call_target="tpu_custom_call" | custom-call | tf_op jit(solution)/shard_map/pallas_call | solution.py:503

commit v5 on v4

--- a/solution.py
+++ b/solution.py
@@ -19,7 +19,8 @@
 LEVELS = 4
 BATCH = 8
 SIDE = 0
-COEF_UNROLL = 2
+COEF_UNROLL = 10
+HALO_CUT = 30
 TINY = 1e-12
 MESH = pl.DeviceIdType.MESH
 bf16 = jnp.bfloat16
@@ -80,8 +81,6 @@
     lrecv,
     halo_send,
     halo_recv,
-    chalo_send,
-    chalo_recv,
     term_send,
     term_recv,
     lev_send,
@@ -115,7 +114,7 @@
     def inside(k):
         return jnp.logical_and(me + k >= 0, me + k < n)
 
-    steps = sorted({abs(k) for k in HALO} | {abs(o) << j for j in range(LEVELS) for o in OFFSETS})
+    steps = sorted({2} | {abs(o) << j for j in range(LEVELS) for o in OFFSETS})
     steps = steps + [-k for k in steps]
     lrecv[...] = jnp.zeros_like(lrecv)
     barrier = pltpu.get_barrier_semaphore()
@@ -250,20 +249,44 @@
             begin(k, copy)
 
     send_level(0)
-    for mine, ref, rows, send, recv in (
-        (own, win, LEAVES, halo_send, halo_recv),
-        (cown, cwin, PAIRS // 2, chalo_send, chalo_recv),
-    ):
-        for num, k in enumerate(HALO):
-            copy = pltpu.make_async_remote_copy(
-                src_ref=mine,
-                dst_ref=ref.at[pl.ds((2 - k) * rows, rows)],
-                send_sem=send.at[num],
-                recv_sem=recv.at[num],
-                device_id=(away(k),),
-                device_id_type=MESH,
-            )
-            begin(k, copy)
+    core = lax.rem(me, 2)
+    sibling = me + 1 - 2 * core
+    chunks = [
+        (own, win, LEAVES, 0, HALO_CUT),
+        (own, win, LEAVES, HALO_CUT, LEAVES - HALO_CUT),
+        (cown, cwin, PAIRS // 2, 0, PAIRS // 2),
+    ]
+
+    def halo_copy(route, part, src, slot, device):
+        _, ref, rows, at, size = chunks[part]
+        return pltpu.make_async_remote_copy(
+            src_ref=src,
+            dst_ref=ref.at[pl.ds(slot * rows + at, size)],
+            send_sem=halo_send.at[route, part],
+            recv_sem=halo_recv.at[route, part],
+            device_id=(device,),
+            device_id_type=MESH,
+        )
+
+    outer = {}
+    to_sibling = []
+
+    def send_halo(part):
+        mine, _, _, at, size = chunks[part]
+        src = mine.at[pl.ds(at, size)]
+        for route, k in enumerate((-2, 2)):
+            copy = halo_copy(route, part, src, 2 - k, away(k))
+            outer[k, part] = copy
+
+            @pl.when(inside(k))
+            def _(copy=copy):
+                copy.start()
+
+        to_sibling.append(halo_copy(2, part, src, 1 + 2 * core, sibling))
+        to_sibling[-1].start()
+
+    send_halo(2)
+    send_halo(0)
 
     for copy in terms:
         copy.wait()
@@ -274,6 +297,8 @@
         lev[j] = rounded(total)
         send_level(j)
 
+    send_halo(1)
+
     def build_points(i, carry):
         at = pl.ds(pl.multiple_of(i * 128, 128), 128)
         c = coords[:, at].astype(f32)
@@ -286,8 +311,28 @@
     stores.append(pltpu.make_async_copy(pts, pts_h, store_sems.at[2]))
     stores[-1].start()
 
-    level_copies = copies[:4] + copies[12:]
-    finish(level_copies)
+    forwards = {}
+
+    def forward_halo(part):
+        _, ref, rows, at, size = chunks[part]
+        src = ref.at[pl.ds((4 - 4 * core) * rows + at, size)]
+        copy = halo_copy(3, part, src, 3 - 2 * core, sibling)
+        forwards[part] = copy
+
+        @pl.when(jnp.logical_and(core == 0, inside(2)))
+        def _():
+            outer[-2, part].wait_recv()
+            copy.start()
+
+        @pl.when(jnp.logical_and(core == 1, inside(-2)))
+        def _():
+            outer[2, part].wait_recv()
+            copy.start()
+
+    forward_halo(2)
+    forward_halo(0)
+    forward_halo(1)
+    finish(copies)
     total = jnp.zeros((8, 64), f32)
     for j in range(LEVELS):
         for num in range(4):
@@ -304,7 +349,29 @@
             for clear in clears(num, k):
                 clear.wait()
 
-    finish(copies[4:12])
+    for copy in to_sibling:
+        copy.wait()
+    for part in range(3):
+        for k in (-2, 2):
+            @pl.when(inside(k))
+            def _(copy=outer[k, part]):
+                copy.wait_send()
+
+        @pl.when(jnp.logical_and(core == 1, inside(2)))
+        def _(copy=outer[-2, part]):
+            copy.wait_recv()
+
+        @pl.when(jnp.logical_and(core == 0, inside(-2)))
+        def _(copy=outer[2, part]):
+            copy.wait_recv()
+
+        @pl.when(inside(2 - 4 * core))
+        def _(copy=forwards[part]):
+            copy.wait_send()
+
+        @pl.when(inside(2 * core - 1))
+        def _(copy=forwards[part]):
+            copy.wait_recv()
 
 
 def matern(u):
@@ -551,10 +618,8 @@
             pltpu.VMEM((8, 3, 8, 128), f32),
             pltpu.VMEM((LEVELS, 8, 128), f32),
             pltpu.VMEM((LEVELS, 4, 8, 128), f32),
-            dma((4,)),
-            dma((4,)),
-            dma((4,)),
-            dma((4,)),
+            dma((4, 3)),
+            dma((4, 3)),
             dma((8,)),
             dma((8,)),
             dma((LEVELS, 4)),

time: 45 us -> 42.5 us (0.944)
  the two profiles are of different devices: /device:TPU:240 before, /device:TPU:253 now
where the time goes in v5:
time: 42.5 us; the launch traced here: 42.3 us
  Pallas kernels  42.3 us (100%)
    pallas_call x1, Pallas kernels, run_field(): pl.pallas_call(field_kernel, out_shape=jax.ShapeDtypeStruct((8, LEAVES *...  23.4 us
    pallas_call x1, Pallas kernels, run_comm(): pl.pallas_call(comm_kernel, out_shape=[jax.ShapeDtypeStruct((5 * LEAVES,...  18.9 us

profile of v5, /device:TPU:253, one launch (start us, length us, event | category | flops | bytes accessed | tf_op | source)
XLA Modules:
  0.0 42.3 jit_solution(4421259282014235019)
XLA Ops:
  0.0 18.9 %shard_map.100 = (bf16[200,16,128]{2,1,0:T(8,128)(2,1)}, bf16[50,16,128]{2,1,0:T(8,128)(2,1)}, bf16[40,128,16]{2,1,0:T(8,128)(2,1)}, f32[8,64]{1,0:T(8,128)}) custom-call(bf16[3,5120]{1,0:T(4,128)(2,1)} %coords_h.1, f32[8,5120]{1,0:T(8,128)} %rhs_h.3, bf16[20,128,128]{2,1,0:T(8,128)(2,1)} %bitcast.10, bf16[20,128,64]{2,1,0:T(8,128)(2,1)} %bitcast.8, ...), custom_call_target="tpu_custom_call" | custom-call | tf_op jit(solution)/shard_map/pallas_call | solution.py:597
  18.9 23.4 %shard_map.101 = f32[8,5120]{1,0:T(8,128)} custom-call(s32[27,40]{1,0:T(8,128)} %bitcast.14, s32[40]{0:T(128)} %counts_h.1, s32[8,40]{1,0:T(8,128)} %bitcast.15, bf16[40,512,64]{2,1,0:T(8,128)(2,1)} %bitcast.7, bf16[20,128,64]{2,1,0:T(8,128)(2,1)} %bitcast.9, bf16[20,128,128]{2,1,0:T(8,128)(2,1)} %bitcast.11, f32[8,5120]{1,0:T(8,128)} %rhs_h.3, ...), custom_call_target="tpu_custom_call" | custom-call | tf_op jit(solution)/shard_map/pallas_call | solution.py:570

commit v6 on v5

--- a/solution.py
+++ b/solution.py
@@ -8,8 +8,8 @@
 from jax.experimental.pallas import tpu as pltpu
 from jax.sharding import PartitionSpec as P
 
-S_RATE = 3.0**0.5 / 0.2
-C_RATE = S_RATE * math.log2(math.e)
+LOG2_E = math.log2(math.e)
+SQ_RATE = 75.0
 NOISE = 0.1
 OFFSETS = (-3, -2, 2, 3)
 HALO = (-2, -1, 1, 2)
@@ -18,7 +18,6 @@
 SLOTS = 27
 LEVELS = 4
 BATCH = 8
-SIDE = 0
 COEF_UNROLL = 10
 HALO_CUT = 30
 TINY = 1e-12
@@ -26,7 +25,6 @@
 bf16 = jnp.bfloat16
 f32 = jnp.float32
 NT = (((1,), (1,)), ((), ()))
-TN = (((0,), (0,)), ((), ()))
 
 
 def rounded(x):
@@ -43,7 +41,7 @@
 
 def norm_pieces(c):
     sq = c * c
-    n2 = sq[0:1] + sq[1:2] + sq[2:3]
+    n2 = SQ_RATE * (sq[0:1] + sq[1:2] + sq[2:3])
     high = rounded(n2)
     mid = rounded(n2 - high)
     low = n2 - high - mid
@@ -131,6 +129,8 @@
     ones2 = jnp.ones((2, 128), f32)
     ones3 = jnp.ones((3, 128), f32)
     zero8 = jnp.zeros((8, 128), f32)
+    zero3 = jnp.zeros((3, 128), f32)
+    zero1 = jnp.zeros((1, 128), f32)
 
     def build(i, carry):
         at = pl.ds(pl.multiple_of(i * 128, 128), 128)
@@ -303,7 +303,10 @@
         at = pl.ds(pl.multiple_of(i * 128, 128), 128)
         c = coords[:, at].astype(f32)
         high, mid, low = norm_pieces(c)
-        tile = jnp.concatenate([zero8, -2.0 * c, ones3, high, mid], axis=0)
+        whole = (-2.0 * SQ_RATE) * c
+        main = rounded(whole)
+        rows = [zero8, main, ones3, high, mid, zero8, whole - main, zero3, low, zero1]
+        tile = jnp.concatenate(rows, axis=0)
         pts[i] = tile.T.astype(bf16)
         return carry
 
@@ -376,8 +379,8 @@
 
 def matern(u):
     u = jnp.maximum(u, TINY)
-    r = u * lax.rsqrt(u)
-    return ((1.0 + S_RATE * r) * jnp.exp2(-C_RATE * r)).astype(bf16)
+    x = u * lax.rsqrt(u)
+    return ((1.0 + x) * jnp.exp2(-LOG2_E * x)).astype(bf16)
 
 
 def expand_coefs(cwin, table, first):
@@ -444,11 +447,8 @@
 
     def distance(leaf, s, g):
         i, a, b = entries(leaf, s)
-        q = jnp.concatenate([win[a], win[b]], axis=1 - SIDE)
-        if SIDE:
-            dist[g] = lax.dot_general(q, pts[i], TN, preferred_element_type=f32)
-        else:
-            dist[g] = dot(pts[i], q)
+        q = jnp.concatenate([win[a], win[b]], axis=1)
+        dist[g] = dot(pts[i], jnp.concatenate([q, q], axis=0))
 
     def values(g):
         block[g] = matern(dist[g])
@@ -461,10 +461,7 @@
         rb = jnp.where(both, win[b], nothing)
         r = jnp.concatenate([ra, rb], axis=1)
         k = block[g]
-        if SIDE:
-            d = dot(r, jnp.concatenate([k[:, :128], k[:, 128:]], axis=0))
-        else:
-            d = dot_nt(r, k)
+        d = dot_nt(r, k)
         at = pl.ds(pl.multiple_of(i * 128, 128), 128)
         out[:, at] += d[:8]
 
@@ -599,7 +596,7 @@
         out_shape=[
             jax.ShapeDtypeStruct((5 * LEAVES, 16, 128), bf16),
             jax.ShapeDtypeStruct((5 * PAIRS // 2, 16, 128), bf16),
-            jax.ShapeDtypeStruct((LEAVES, 128, 16), bf16),
+            jax.ShapeDtypeStruct((LEAVES, 128, 32), bf16),
             jax.ShapeDtypeStruct((8, 64), f32),
         ],
         in_specs=[hbm] * len(arrays),
@@ -609,7 +606,7 @@
             dma((6,)),
             pltpu.VMEM((LEAVES, 16, 128), bf16),
             pltpu.VMEM((PAIRS // 2, 16, 128), bf16),
-            pltpu.VMEM((LEAVES, 128, 16), bf16),
+            pltpu.VMEM((LEAVES, 128, 32), bf16),
             pltpu.VMEM((8, 64), f32),
             pltpu.VMEM((LEAVES, 16, 128), bf16),
             dma((4,)),

time: 42.5 us -> 41.4 us (0.974)
  the two profiles are of different devices: /device:TPU:253 before, /device:TPU:240 now
where the time goes in v6:
time: 41.4 us; the launch traced here: 41.2 us
  Pallas kernels  41.2 us (100%)
    pallas_call x1, Pallas kernels, run_field(): pl.pallas_call(field_kernel, out_shape=jax.ShapeDtypeStruct((8, LEAVES *...  21.5 us
    pallas_call x1, Pallas kernels, run_comm(): pl.pallas_call(comm_kernel, out_shape=[jax.ShapeDtypeStruct((5 * LEAVES,...  19.7 us

profile of v6, /device:TPU:240, one launch (start us, length us, event | category | flops | bytes accessed | tf_op | source)
XLA Modules:
  0.0 41.2 jit_solution(17420908727402947389)
XLA Ops:
  0.0 19.7 %shard_map.100 = (bf16[200,16,128]{2,1,0:T(8,128)(2,1)}, bf16[50,16,128]{2,1,0:T(8,128)(2,1)}, bf16[40,128,32]{2,1,0:T(8,128)(2,1)}, f32[8,64]{1,0:T(8,128)}) custom-call(bf16[3,5120]{1,0:T(4,128)(2,1)} %coords_h.1, f32[8,5120]{1,0:T(8,128)} %rhs_h.3, bf16[20,128,128]{2,1,0:T(8,128)(2,1)} %bitcast.10, bf16[20,128,64]{2,1,0:T(8,128)(2,1)} %bitcast.8, ...), custom_call_target="tpu_custom_call" | custom-call | tf_op jit(solution)/shard_map/pallas_call | solution.py:594
  19.7 21.5 %shard_map.101 = f32[8,5120]{1,0:T(8,128)} custom-call(s32[27,40]{1,0:T(8,128)} %bitcast.14, s32[40]{0:T(128)} %counts_h.1, s32[8,40]{1,0:T(8,128)} %bitcast.15, bf16[40,512,64]{2,1,0:T(8,128)(2,1)} %bitcast.7, bf16[20,128,64]{2,1,0:T(8,128)(2,1)} %bitcast.9, bf16[20,128,128]{2,1,0:T(8,128)(2,1)} %bitcast.11, f32[8,5120]{1,0:T(8,128)} %rhs_h.3, ...), custom_call_target="tpu_custom_call" | custom-call | tf_op jit(solution)/shard_map/pallas_call | solution.py:567

commit v7 on v6

--- a/solution.py
+++ b/solution.py
@@ -19,7 +19,7 @@
 LEVELS = 4
 BATCH = 8
 COEF_UNROLL = 10
-HALO_CUT = 30
+HALO_CUT = 26
 TINY = 1e-12
 MESH = pl.DeviceIdType.MESH
 bf16 = jnp.bfloat16
@@ -492,7 +492,7 @@
     far_sums, far_field = prepare_far()
 
     def both_steps(t, carry):
-        return near_step(carry, {1: lambda: far_sums(t), 7: lambda: far_field(t)})
+        return near_step(carry, {0: lambda: far_sums(t), 6: lambda: far_field(t)})
 
     def far_step(t, carry):
         far_sums(t)

time: 41.4 us -> 40.6 us (0.981)
  the two profiles are of different devices: /device:TPU:240 before, /device:TPU:257 now
where the time goes in v7:
time: 40.6 us; the launch traced here: 39.9 us
  Pallas kernels  39.9 us (98%)
    pallas_call x1, Pallas kernels, run_field(): pl.pallas_call(field_kernel, out_shape=jax.ShapeDtypeStruct((8, LEAVES *...  20.8 us
    pallas_call x1, Pallas kernels, run_comm(): pl.pallas_call(comm_kernel, out_shape=[jax.ShapeDtypeStruct((5 * LEAVES,...  19.1 us

profile of v7, /device:TPU:257, one launch (start us, length us, event | category | flops | bytes accessed | tf_op | source)
XLA Modules:
  0.0 39.9 jit_solution(15606058827716518497)
XLA Ops:
  0.0 19.1 %shard_map.100 = (bf16[200,16,128]{2,1,0:T(8,128)(2,1)}, bf16[50,16,128]{2,1,0:T(8,128)(2,1)}, bf16[40,128,32]{2,1,0:T(8,128)(2,1)}, f32[8,64]{1,0:T(8,128)}) custom-call(bf16[3,5120]{1,0:T(4,128)(2,1)} %coords_h.1, f32[8,5120]{1,0:T(8,128)} %rhs_h.3, bf16[20,128,128]{2,1,0:T(8,128)(2,1)} %bitcast.10, bf16[20,128,64]{2,1,0:T(8,128)(2,1)} %bitcast.8, ...), custom_call_target="tpu_custom_call" | custom-call | tf_op jit(solution)/shard_map/pallas_call | solution.py:594
  19.1 20.8 %shard_map.101 = f32[8,5120]{1,0:T(8,128)} custom-call(s32[27,40]{1,0:T(8,128)} %bitcast.14, s32[40]{0:T(128)} %counts_h.1, s32[8,40]{1,0:T(8,128)} %bitcast.15, bf16[40,512,64]{2,1,0:T(8,128)(2,1)} %bitcast.7, bf16[20,128,64]{2,1,0:T(8,128)(2,1)} %bitcast.9, bf16[20,128,128]{2,1,0:T(8,128)(2,1)} %bitcast.11, f32[8,5120]{1,0:T(8,128)} %rhs_h.3, ...), custom_call_target="tpu_custom_call" | custom-call | tf_op jit(solution)/shard_map/pallas_call | solution.py:567
